TPU v7x, 256 devices: a whole 4x4x8 slice. The times are simulated.
256 devices in a mesh: dp: 16 (over z, core), seq: 16 (over y, x).
Axes of the slice: x: 4, y: 4, z: 8, core: 2. Of those that a mesh axis runs over, the one named last changes fastest.
Arguments:
- query_states: bfloat16 [32768, 8192], P(('dp', 'seq')), parts along dimension 0, may hold values from -140 to 140
- key_states: bfloat16 [32768, 1024], P(('dp', 'seq')), parts along dimension 0, may hold values from -7 to 7
- value_states: bfloat16 [32768, 1024], P(('dp', 'seq')), parts along dimension 0, may hold values from -6 to 6
- output_grad: bfloat16 [32768, 8192], P(('dp', 'seq')), parts along dimension 0, may hold values from -6 to 6
- document_lengths: int32 [512], P('dp'), parts along dimension 0, may hold values from 1 to 191, as said below
- document_owners: int32 [512], P('dp'), parts along dimension 0, may hold values from 0 to 15, as said below
- block_table: int32 [256, 16], P('dp'), parts along dimension 0, may hold values from 0 to 1, as said below
Outputs:
- attention_out: bfloat16 [49152, 8192], P(('dp', 'seq')), parts along dimension 0
- query_grad: bfloat16 [49152, 8192], P(('dp', 'seq')), parts along dimension 0
- key_grad: bfloat16 [49152, 1024], P(('dp', 'seq')), parts along dimension 0
- value_grad: bfloat16 [49152, 1024], P(('dp', 'seq')), parts along dimension 0
There are 16 independent parts, one for each index of `dp`. A program takes and returns all parts, laid end to end along the dimension named above; each array names one. Nothing has to cross between parts.
Inputs may be any that keep to these rules, and one draw needn't show every extreme that they name: `document_lengths`: the lengths sum to 2048; some document has exactly 191 tokens. `document_owners`: owners do not fall along the documents; every device owns one to three consecutive documents, which hold at most 192 tokens together, exactly 192 for some owner; all tokens of device d's documents lie at positions from d * 128 - 128 // 4 to (d + 1) * 128 + 128 // 4 - 1. `block_table`: the diagonal is 1.
All inputs are finite; a program needn't handle non-finite values.
Results may differ from a plain program's by a relative error of at most 0.0051.
Values may be sent and summed in bfloat16 or wider, within the bound.
A program may use at most 128 MiB of HBM per device.

v0:
```python
import jax
import jax.numpy as jnp
from jax import lax
from jax.sharding import PartitionSpec as P

HEADS = 64
KV_HEADS = 8
HEAD_DIM = 128
BLOCK = 128
CAP = 192


def slot_layout(document_lengths, document_owners, total):
    doc_count = document_lengths.shape[0]
    starts = jnp.cumsum(document_lengths) - document_lengths
    position = jnp.arange(total, dtype=jnp.int32)
    inside = (position[:, None] >= starts[None, :]).astype(jnp.int32)
    doc_ids = jnp.sum(inside, axis=1) - 1
    numbers = jnp.arange(doc_count, dtype=jnp.int32)
    shared = (document_owners[:, None] == document_owners[None, :]) & (
        numbers[None, :] < numbers[:, None]
    )
    offsets = jnp.sum(jnp.where(shared, document_lengths[None, :], 0), axis=1)
    doc_slot = document_owners * CAP + offsets - starts
    picked = doc_ids[:, None] == numbers[None, :]
    token_slot = jnp.sum(jnp.where(picked, doc_slot[None, :], 0), axis=1) + position
    return (doc_ids, token_slot)


def table_mask(block_table, row_blocks, col_blocks):
    numbers = jnp.arange(block_table.shape[0], dtype=jnp.int32)
    left_hot = (row_blocks[:, None] == numbers[None, :]).astype(jnp.float32)
    right_hot = (col_blocks[:, None] == numbers[None, :]).astype(jnp.float32)
    return jnp.dot(jnp.dot(left_hot, block_table.astype(jnp.float32)), right_hot.T) > 0.5


def attend(query_block, key_block, value_block, grad_block, allowed):
    inv_root = query_block.shape[-1] ** (-0.5)
    scores = (
        jnp.einsum("rkpd,wkd->kprw", query_block, key_block, preferred_element_type=jnp.float32)
        * inv_root
    )
    scores = jnp.where(allowed[None, None], scores, -jnp.inf)
    highest = jnp.max(scores, axis=-1, keepdims=True)
    raised = jnp.exp(scores - highest)
    summed = jnp.sum(raised, axis=-1, keepdims=True)
    prob_full = raised / summed
    prob_half = prob_full.astype(jnp.bfloat16)
    output_block = jnp.einsum(
        "kprw,wkd->rkpd", prob_half, value_block, preferred_element_type=jnp.float32
    ).astype(jnp.bfloat16)
    prob_grad = jnp.einsum(
        "rkpd,wkd->kprw", grad_block, value_block, preferred_element_type=jnp.float32
    )
    row_delta = jnp.sum(prob_full * prob_grad, axis=-1, keepdims=True)
    score_grad = (prob_full * (prob_grad - row_delta)).astype(jnp.bfloat16)
    query_grad = (
        jnp.einsum("kprw,wkd->rkpd", score_grad, key_block, preferred_element_type=jnp.float32)
        * inv_root
    ).astype(jnp.bfloat16)
    key_grad = (
        jnp.einsum("kprw,rkpd->wkd", score_grad, query_block, preferred_element_type=jnp.float32)
        * inv_root
    )
    value_grad = jnp.einsum(
        "kprw,rkpd->wkd", prob_half, grad_block, preferred_element_type=jnp.float32
    )
    return (output_block, query_grad, key_grad, value_grad)


def local(
    query_states,
    key_states,
    value_states,
    output_grad,
    document_lengths,
    document_owners,
    block_table,
):
    devices = lax.axis_size("seq")
    tok_rows = query_states.shape[0]
    total = tok_rows * devices
    heads_dev = HEADS // devices
    group_size = HEADS // KV_HEADS
    kv_dev = max(1, heads_dev // group_size)
    copies = devices * kv_dev // KV_HEADS
    per_kv = heads_dev // kv_dev
    doc_ids, token_slot = slot_layout(document_lengths, document_owners, total)
    position = jnp.arange(total, dtype=jnp.int32)
    source = jnp.full((devices * CAP,), -1, jnp.int32).at[token_slot].set(position)
    filled = source >= 0
    safe_source = jnp.maximum(source, 0)

    def to_slots(rows):
        return jnp.where(filled[:, None], rows[safe_source], jnp.zeros((), rows.dtype))

    def widen(rows):
        return jnp.broadcast_to(
            rows.reshape(tok_rows, KV_HEADS, 1, HEAD_DIM), (tok_rows, KV_HEADS, copies, HEAD_DIM)
        ).reshape(tok_rows, KV_HEADS * copies * HEAD_DIM)

    head_queries, head_grads, head_keys, head_values = (
        lax.all_to_all(query_states, "seq", split_axis=1, concat_axis=0, tiled=True),
        lax.all_to_all(output_grad, "seq", split_axis=1, concat_axis=0, tiled=True),
        lax.all_to_all(widen(key_states), "seq", split_axis=1, concat_axis=0, tiled=True),
        lax.all_to_all(widen(value_states), "seq", split_axis=1, concat_axis=0, tiled=True),
    )
    look = (CAP + 127) // 128 * 128
    qblock = min(512, total)
    span = qblock + look
    query_four = head_queries.reshape(total, kv_dev, per_kv, HEAD_DIM)
    grad_four = head_grads.reshape(total, kv_dev, per_kv, HEAD_DIM)
    pad_keys = jnp.concatenate(
        [
            jnp.zeros((look, kv_dev, HEAD_DIM), jnp.bfloat16),
            head_keys.reshape(total, kv_dev, HEAD_DIM),
        ],
        axis=0,
    )
    pad_values = jnp.concatenate(
        [
            jnp.zeros((look, kv_dev, HEAD_DIM), jnp.bfloat16),
            head_values.reshape(total, kv_dev, HEAD_DIM),
        ],
        axis=0,
    )
    pad_docs = jnp.concatenate([jnp.full((look,), -2, jnp.int32), doc_ids], axis=0)
    pad_position = jnp.arange(-look, total, dtype=jnp.int32)

    def step(block_number, carry):
        out_acc, qgrad_acc, kgrad_acc, vgrad_acc = carry
        first = block_number * qblock
        query_part = lax.dynamic_slice_in_dim(query_four, first, qblock, 0)
        grad_part = lax.dynamic_slice_in_dim(grad_four, first, qblock, 0)
        key_part = lax.dynamic_slice_in_dim(pad_keys, first, span, 0)
        value_part = lax.dynamic_slice_in_dim(pad_values, first, span, 0)
        row_docs = lax.dynamic_slice_in_dim(doc_ids, first, qblock, 0)
        col_docs = lax.dynamic_slice_in_dim(pad_docs, first, span, 0)
        row_pos = lax.dynamic_slice_in_dim(position, first, qblock, 0)
        col_pos = lax.dynamic_slice_in_dim(pad_position, first, span, 0)
        allowed = (row_docs[:, None] == col_docs[None, :]) & (col_pos[None, :] <= row_pos[:, None])
        allowed = allowed & table_mask(
            block_table, row_pos // BLOCK, jnp.maximum(col_pos, 0) // BLOCK
        )
        out_block, qgrad_block, kgrad_block, vgrad_block = attend(
            query_part, key_part, value_part, grad_part, allowed
        )
        out_acc = lax.dynamic_update_slice_in_dim(
            out_acc, out_block.reshape(qblock, heads_dev * HEAD_DIM), first, 0
        )
        qgrad_acc = lax.dynamic_update_slice_in_dim(
            qgrad_acc, qgrad_block.reshape(qblock, heads_dev * HEAD_DIM), first, 0
        )
        kgrad_acc = lax.dynamic_update_slice_in_dim(
            kgrad_acc, lax.dynamic_slice_in_dim(kgrad_acc, first, span, 0) + kgrad_block, first, 0
        )
        vgrad_acc = lax.dynamic_update_slice_in_dim(
            vgrad_acc, lax.dynamic_slice_in_dim(vgrad_acc, first, span, 0) + vgrad_block, first, 0
        )
        return (out_acc, qgrad_acc, kgrad_acc, vgrad_acc)

    initial = (
        jnp.zeros((total, heads_dev * HEAD_DIM), jnp.bfloat16),
        jnp.zeros((total, heads_dev * HEAD_DIM), jnp.bfloat16),
        jnp.zeros((look + total, kv_dev, HEAD_DIM), jnp.float32),
        jnp.zeros((look + total, kv_dev, HEAD_DIM), jnp.float32),
    )
    out_rows, qgrad_rows, kgrad_pad, vgrad_pad = lax.fori_loop(0, total // qblock, step, initial)
    kgrad_rows = kgrad_pad[look:].reshape(total, kv_dev * HEAD_DIM)
    vgrad_rows = vgrad_pad[look:].reshape(total, kv_dev * HEAD_DIM)
    attention_out, query_grad = (
        lax.all_to_all(to_slots(out_rows), "seq", split_axis=0, concat_axis=1, tiled=True),
        lax.all_to_all(to_slots(qgrad_rows), "seq", split_axis=0, concat_axis=1, tiled=True),
    )
    key_parts, value_parts = (
        lax.all_to_all(to_slots(kgrad_rows), "seq", split_axis=0, concat_axis=1, tiled=True),
        lax.all_to_all(to_slots(vgrad_rows), "seq", split_axis=0, concat_axis=1, tiled=True),
    )
    key_grad = (
        key_parts.reshape(CAP, KV_HEADS, copies, HEAD_DIM)
        .sum(axis=2)
        .reshape(CAP, KV_HEADS * HEAD_DIM)
        .astype(jnp.bfloat16)
    )
    value_grad = (
        value_parts.reshape(CAP, KV_HEADS, copies, HEAD_DIM)
        .sum(axis=2)
        .reshape(CAP, KV_HEADS * HEAD_DIM)
        .astype(jnp.bfloat16)
    )
    return (attention_out, query_grad, key_grad, value_grad)


def solution(mesh):
    return jax.shard_map(
        local,
        mesh=mesh,
        in_specs=(
            P(("dp", "seq"), None),
            P(("dp", "seq"), None),
            P(("dp", "seq"), None),
            P(("dp", "seq"), None),
            P("dp"),
            P("dp"),
            P("dp", None),
        ),
        out_specs=(
            P(("dp", "seq"), None),
            P(("dp", "seq"), None),
            P(("dp", "seq"), None),
            P(("dp", "seq"), None),
        ),
        check_vma=False,
    )
```

profile of v0, /device:TPU:174, one launch (start us, length us, event | category | flops | bytes accessed | tf_op | source)
XLA Modules:
  0.0 480.1 jit_solution(14279355519092684851)
XLA Ops:
  2.8 7.3 %all-to-all-start = ((bf16[128,16,128]{0,2,1:T(8,128)(2,1)}), bf16[128,16,128]{0,2,1:T(8,128)(2,1)S(1)}, u32[]{:S(2)}, u32[]{:S(2)}) async-start(bf16[128,16,128]{0,2,1:T(8,128)(2,1)} %bitcast.31), calls=%async_computation | async-start | bytes 1048576 | tf_op jit(solution)/shard_map/all_to_all | solution.py:106
  10.2 8.0 %all-to-all-done = bf16[128,16,128]{0,2,1:T(8,128)(2,1)S(1)} async-done(((bf16[128,16,128]{0,2,1:T(8,128)(2,1)}), bf16[128,16,128]{0,2,1:T(8,128)(2,1)S(1)}, u32[]{:S(2)}, u32[]{:S(2)}) %all-to-all-start) | async-done | bytes 524320 | tf_op jit(solution)/shard_map/all_to_all | solution.py:106
  19.1 7.0 %all-to-all-start.1 = ((bf16[128,16,128]{2,0,1:T(8,128)(2,1)}), bf16[128,16,128]{2,0,1:T(8,128)(2,1)S(1)}, u32[]{:S(2)}, u32[]{:S(2)}) async-start(bf16[128,16,128]{2,0,1:T(8,128)(2,1)} %bitcast.251), calls=%async_computation.1 | async-start | bytes 1048576 | tf_op jit(solution)/shard_map/all_to_all | solution.py:105
  33.2 7.2 %all-to-all-start.2 = ((bf16[128,16,512]{0,2,1:T(8,128)(2,1)}), bf16[128,16,512]{0,2,1:T(8,128)(2,1)S(1)}, u32[]{:S(2)}, u32[]{:S(2)}) async-start(bf16[128,16,512]{0,2,1:T(8,128)(2,1)} %bitcast.245), calls=%async_computation.2 | async-start | bytes 4194304 | tf_op jit(solution)/shard_map/all_to_all | solution.py:103
  44.4 19.7 %all-to-all-done.2 = bf16[128,16,512]{0,2,1:T(8,128)(2,1)S(1)} async-done(((bf16[128,16,512]{0,2,1:T(8,128)(2,1)}), bf16[128,16,512]{0,2,1:T(8,128)(2,1)S(1)}, u32[]{:S(2)}, u32[]{:S(2)}) %all-to-all-start.2) | async-done | bytes 2097184 | tf_op jit(solution)/shard_map/all_to_all | solution.py:103
  64.1 8.8 %all-to-all-start.3 = ((bf16[128,16,512]{0,2,1:T(8,128)(2,1)}), bf16[128,16,512]{0,2,1:T(8,128)(2,1)}, u32[]{:S(2)}, u32[]{:S(2)}) async-start(bf16[128,16,512]{0,2,1:T(8,128)(2,1)} %bitcast.244), calls=%async_computation.3 | async-start | bytes 4194304 | tf_op jit(solution)/shard_map/all_to_all | solution.py:104
  73.7 8.1 %scatter_custom_fusion = s32[3072]{0:T(1024)S(1)} fusion(s32[2048]{0:T(1024)S(1)} %bitcast.255, s32[2048]{0:T(1024)S(1)} %iota.43, s32[]{:T(128)} %constant.174.clone.1), kind=kCustom, calls=%fused_computation.101 | custom fusion | bytes 12292 | tf_op jit(solution)/shard_map/scatter | solution.py:90
  107.6 192.2 %while.22 = (s32[]{:T(128)}, bf16[2048,512]{1,0:T(8,128)(2,1)}, bf16[2048,512]{1,0:T(8,128)(2,1)}, f32[2304,1,128]{2,0,1:T(8,128)}, f32[2304,1,128]{2,0,1:T(8,12...) while((s32[]{:T(128)}, bf16[2048,512]{1,0:T(8,128)(2,1)}, ...), condition=%wide.region_9.10_spmd, body=%wide.region_5.9_spmd.sunk | while | flops 2479026432 | bytes 106185568 | solution.py:168
  124.4 5.7 %fusion.101 = bf16[128,4,512]{2,0,1:T(8,128)(2,1)} fusion(bf16[2304,1,128]{2,0,1:T(8,128)(2,1)} %get-tuple-element.638, s32[]{:T(128)S(6)} %select_n.165, f32[4,512]{1,0:T(4,128)S(1)} %fusion.97, f32[4,512]{1,0:T(4,128)S(1)} %get-tuple-element.588, f32[768,512,4]{1,0,2:T(8,128)} %copy-done.2, pred[512,768]{0,1:T(8,128)(4,1)} %copy-done.4), kind=kOutput, calls=%fused_computation.24.clone.1 | convolution fusion | flops 410779648 | bytes 7421956 | tf_op jit(solution)/shard_map/while/body/eval_jaxpr/kprw,wkd->rkpd/dot_general | solution.py:49
  138.1 5.8 %fusion.102 = f32[768,1,128]{0,2,1:T(8,128)} fusion(f32[768,1,128]{0,2,1:T(8,128)} %copy.177, bf16[2048,1,4,128]{0,3,2,1:T(8,128)(2,1)} %get-tuple-element.646, s32[]{:T(128)S(6)} %select_n.166, f32[4,512]{1,0:T(4,128)S(1)} %fusion.97, f32[4,512]{1,0:T(4,128)S(1)} %get-tuple-element.588, f32[768,512,4]{1,0,2:T(8,128)} %copy-done.2, ...), kind=kOutput, calls=%fused_computation.27.clone.1 | convolution fusion | flops 410615808 | bytes 8011780 | tf_op jit(solution)/shard_map/while/body/eval_jaxpr/kprw,rkpd->wkd/dot_general | solution.py:65
  172.4 5.7 %fusion.101 = bf16[128,4,512]{2,0,1:T(8,128)(2,1)} fusion(bf16[2304,1,128]{2,0,1:T(8,128)(2,1)} %get-tuple-element.638, s32[]{:T(128)S(6)} %select_n.165, f32[4,512]{1,0:T(4,128)S(1)} %fusion.97, f32[4,512]{1,0:T(4,128)S(1)} %get-tuple-element.588, f32[768,512,4]{1,0,2:T(8,128)} %copy-done.2, pred[512,768]{0,1:T(8,128)(4,1)} %copy-done.4), kind=kOutput, calls=%fused_computation.24.clone.1 | convolution fusion | flops 410779648 | bytes 7421956 | tf_op jit(solution)/shard_map/while/body/eval_jaxpr/kprw,wkd->rkpd/dot_general | solution.py:49
  186.1 5.8 %fusion.102 = f32[768,1,128]{0,2,1:T(8,128)} fusion(f32[768,1,128]{0,2,1:T(8,128)} %copy.177, bf16[2048,1,4,128]{0,3,2,1:T(8,128)(2,1)} %get-tuple-element.646, s32[]{:T(128)S(6)} %select_n.166, f32[4,512]{1,0:T(4,128)S(1)} %fusion.97, f32[4,512]{1,0:T(4,128)S(1)} %get-tuple-element.588, f32[768,512,4]{1,0,2:T(8,128)} %copy-done.2, ...), kind=kOutput, calls=%fused_computation.27.clone.1 | convolution fusion | flops 410615808 | bytes 8011780 | tf_op jit(solution)/shard_map/while/body/eval_jaxpr/kprw,rkpd->wkd/dot_general | solution.py:65
  220.5 5.7 %fusion.101 = bf16[128,4,512]{2,0,1:T(8,128)(2,1)} fusion(bf16[2304,1,128]{2,0,1:T(8,128)(2,1)} %get-tuple-element.638, s32[]{:T(128)S(6)} %select_n.165, f32[4,512]{1,0:T(4,128)S(1)} %fusion.97, f32[4,512]{1,0:T(4,128)S(1)} %get-tuple-element.588, f32[768,512,4]{1,0,2:T(8,128)} %copy-done.2, pred[512,768]{0,1:T(8,128)(4,1)} %copy-done.4), kind=kOutput, calls=%fused_computation.24.clone.1 | convolution fusion | flops 410779648 | bytes 7421956 | tf_op jit(solution)/shard_map/while/body/eval_jaxpr/kprw,wkd->rkpd/dot_general | solution.py:49
  234.2 5.8 %fusion.102 = f32[768,1,128]{0,2,1:T(8,128)} fusion(f32[768,1,128]{0,2,1:T(8,128)} %copy.177, bf16[2048,1,4,128]{0,3,2,1:T(8,128)(2,1)} %get-tuple-element.646, s32[]{:T(128)S(6)} %select_n.166, f32[4,512]{1,0:T(4,128)S(1)} %fusion.97, f32[4,512]{1,0:T(4,128)S(1)} %get-tuple-element.588, f32[768,512,4]{1,0,2:T(8,128)} %copy-done.2, ...), kind=kOutput, calls=%fused_computation.27.clone.1 | convolution fusion | flops 410615808 | bytes 8011780 | tf_op jit(solution)/shard_map/while/body/eval_jaxpr/kprw,rkpd->wkd/dot_general | solution.py:65
  282.2 5.8 %fusion.102 = f32[768,1,128]{0,2,1:T(8,128)} fusion(f32[768,1,128]{0,2,1:T(8,128)} %copy.177, bf16[2048,1,4,128]{0,3,2,1:T(8,128)(2,1)} %get-tuple-element.646, s32[]{:T(128)S(6)} %select_n.166, f32[4,512]{1,0:T(4,128)S(1)} %fusion.97, f32[4,512]{1,0:T(4,128)S(1)} %get-tuple-element.588, f32[768,512,4]{1,0,2:T(8,128)} %copy-done.2, ...), kind=kOutput, calls=%fused_computation.27.clone.1 | convolution fusion | flops 410615808 | bytes 8011780 | tf_op jit(solution)/shard_map/while/body/eval_jaxpr/kprw,rkpd->wkd/dot_general | solution.py:65
  301.5 11.1 %gather_fusion.3 = f32[3072,128]{1,0:T(8,128)} fusion(f32[2048,128]{1,0:T(8,128)S(1)} %get-tuple-element.484, s32[3072]{0:T(1024)S(1)} %copy-done.8), kind=kCustom, calls=%fused_computation.3 | custom fusion | bytes 3158016 | tf_op jit(solution)/shard_map/gather | solution.py:95
  312.6 10.9 %gather_fusion.2 = f32[3072,128]{1,0:T(8,128)} fusion(f32[2048,128]{1,0:T(8,128)S(1)} %get-tuple-element.485, s32[3072]{0:T(1024)S(1)} %copy-done.8), kind=kCustom, calls=%fused_computation.2 | custom fusion | bytes 3158016 | tf_op jit(solution)/shard_map/gather | solution.py:95
  326.1 26.7 %all_to_all.122 = f32[16,192,128]{2,1,0:T(8,128)} all-to-all(f32[16,192,128]{2,1,0:T(8,128)S(1)} %get-tuple-element.481), channel_id=1, replica_groups=mesh['dp'=16,'seq'=16] {'seq'}, dimensions={0} | all-to-all | bytes 3145728 | tf_op jit(solution)/shard_map/all_to_all | solution.py:176
  352.8 7.8 %all-to-all-start.7 = ((f32[16,192,128]{2,1,0:T(8,128)}), f32[16,192,128]{2,1,0:T(8,128)}, u32[]{:S(2)}, u32[]{:S(2)}) async-start(f32[16,192,128]{2,1,0:T(8,128)} %get-tuple-element.480), calls=%async_computation.7 | async-start | bytes 3145728 | tf_op jit(solution)/shard_map/all_to_all | solution.py:177
  360.6 15.4 %gather_fusion.1 = bf16[3072,512]{1,0:T(8,128)(2,1)} fusion(bf16[2048,512]{1,0:T(8,128)(2,1)} %get-tuple-element.379, s32[3072]{0:T(1024)S(1)} %copy-done.8), kind=kCustom, calls=%fused_computation.1 | custom fusion | bytes 6303744 | tf_op jit(solution)/shard_map/gather | solution.py:95
  376.0 13.3 %gather_fusion = bf16[3072,512]{1,0:T(8,128)(2,1)} fusion(bf16[2048,512]{1,0:T(8,128)(2,1)S(1)} %copy-done.3, s32[3072]{0:T(1024)S(1)} %copy-done.8), kind=kCustom, calls=%fused_computation | custom fusion | bytes 6303744 | tf_op jit(solution)/shard_map/gather | solution.py:95
  393.6 41.6 %all_to_all.123 = bf16[16,192,512]{2,1,0:T(8,128)(2,1)} all-to-all(bf16[16,192,512]{2,1,0:T(8,128)(2,1)S(1)} %get-tuple-element.483), channel_id=1, replica_groups=mesh['dp'=16,'seq'=16] {'seq'}, dimensions={0} | all-to-all | bytes 6291456 | tf_op jit(solution)/shard_map/all_to_all | solution.py:172
  435.1 7.4 %all-to-all-start.5 = ((bf16[16,192,512]{2,1,0:T(8,128)(2,1)}), bf16[16,192,512]{2,1,0:T(8,128)(2,1)S(1)}, u32[]{:S(2)}, u32[]{:S(2)}) async-start(bf16[16,192,512]{2,1,0:T(8,128)(2,1)} %get-tuple-element.482), calls=%async_computation.5 | async-start | bytes 6291456 | tf_op jit(solution)/shard_map/all_to_all | solution.py:173
  449.4 28.6 %all-to-all-done.5 = bf16[16,192,512]{2,1,0:T(8,128)(2,1)S(1)} async-done(((bf16[16,192,512]{2,1,0:T(8,128)(2,1)}), bf16[16,192,512]{2,1,0:T(8,128)(2,1)S(1)}, u32[]{:S(2)}, u32[]{:S(2)}) %all-to-all-start.5) | async-done | bytes 3145760 | tf_op jit(solution)/shard_map/all_to_all | solution.py:173
  (173 shorter events, 209.9 us)
Async XLA Ops:
  0.6 9.5 %copy-start = (bf16[128,1024]{1,0:T(8,128)(2,1)S(1)}, bf16[128,1024]{1,0:T(8,128)(2,1)}, u32[]{:S(2)}) copy-start(bf16[128,1024]{1,0:T(8,128)(2,1)} %param.10) | copy-start | bytes 786436
  0.6 25.4 %copy-start.7 = (bf16[128,8192]{1,0:T(8,128)(2,1)S(1)}, bf16[128,8192]{1,0:T(8,128)(2,1)}, u32[]{:S(2)}) copy-start(bf16[128,8192]{1,0:T(8,128)(2,1)} %param.9) | copy-start | bytes 6291460
  2.8 15.3 %all-to-all-start = ((bf16[128,16,128]{0,2,1:T(8,128)(2,1)}), bf16[128,16,128]{0,2,1:T(8,128)(2,1)S(1)}, u32[]{:S(2)}, u32[]{:S(2)}) async-start(bf16[128,16,128]{0,2,1:T(8,128)(2,1)} %bitcast.31), calls=%async_computation | async-start | bytes 1048576 | tf_op jit(solution)/shard_map/all_to_all | solution.py:106
  19.1 14.1 %all-to-all-start.1 = ((bf16[128,16,128]{2,0,1:T(8,128)(2,1)}), bf16[128,16,128]{2,0,1:T(8,128)(2,1)S(1)}, u32[]{:S(2)}, u32[]{:S(2)}) async-start(bf16[128,16,128]{2,0,1:T(8,128)(2,1)} %bitcast.251), calls=%async_computation.1 | async-start | bytes 1048576 | tf_op jit(solution)/shard_map/all_to_all | solution.py:105
  33.2 31.0 %all-to-all-start.2 = ((bf16[128,16,512]{0,2,1:T(8,128)(2,1)}), bf16[128,16,512]{0,2,1:T(8,128)(2,1)S(1)}, u32[]{:S(2)}, u32[]{:S(2)}) async-start(bf16[128,16,512]{0,2,1:T(8,128)(2,1)} %bitcast.245), calls=%async_computation.2 | async-start | bytes 4194304 | tf_op jit(solution)/shard_map/all_to_all | solution.py:103
  44.4 28.5 %copy-start.11 = (s32[32]{0:T(128)S(1)}, s32[32]{0:T(128)}, u32[]{:S(2)}) copy-start(s32[32]{0:T(128)} %param.13) | copy-start | bytes 388
  44.4 28.8 %copy-start.10 = (s32[16,16]{1,0:T(8,128)S(1)}, s32[16,16]{1,0:T(8,128)}, u32[]{:S(2)}) copy-start(s32[16,16]{1,0:T(8,128)} %param.15) | copy-start | bytes 3076
  44.4 28.8 %copy-start.12 = (s32[32]{0:T(128)S(1)}, s32[32]{0:T(128)}, u32[]{:S(2)}) copy-start(s32[32]{0:T(128)} %param.14) | copy-start | bytes 388
  64.1 33.0 %all-to-all-start.3 = ((bf16[128,16,512]{0,2,1:T(8,128)(2,1)}), bf16[128,16,512]{0,2,1:T(8,128)(2,1)}, u32[]{:S(2)}, u32[]{:S(2)}) async-start(bf16[128,16,512]{0,2,1:T(8,128)(2,1)} %bitcast.244), calls=%async_computation.3 | async-start | bytes 4194304 | tf_op jit(solution)/shard_map/all_to_all | solution.py:104
  109.4 3.8 copy-start.4
  111.8 5.2 %copy-start.2 = (f32[768,512,4]{1,0,2:T(8,128)}, f32[768,512,4]{1,0,2:T(8,128)S(1)}, u32[]{:S(2)}) copy-start(f32[768,512,4]{1,0,2:T(8,128)S(1)} %get-tuple-element.587) | copy-start | bytes 18874372 | tf_op jit(solution)/shard_map/while
  157.4 3.8 copy-start.4
  159.9 5.2 %copy-start.2 = (f32[768,512,4]{1,0,2:T(8,128)}, f32[768,512,4]{1,0,2:T(8,128)S(1)}, u32[]{:S(2)}) copy-start(f32[768,512,4]{1,0,2:T(8,128)S(1)} %get-tuple-element.587) | copy-start | bytes 18874372 | tf_op jit(solution)/shard_map/while
  205.5 3.8 copy-start.4
  207.9 5.2 %copy-start.2 = (f32[768,512,4]{1,0,2:T(8,128)}, f32[768,512,4]{1,0,2:T(8,128)S(1)}, u32[]{:S(2)}) copy-start(f32[768,512,4]{1,0,2:T(8,128)S(1)} %get-tuple-element.587) | copy-start | bytes 18874372 | tf_op jit(solution)/shard_map/while
  253.5 3.8 copy-start.4
  256.0 5.2 %copy-start.2 = (f32[768,512,4]{1,0,2:T(8,128)}, f32[768,512,4]{1,0,2:T(8,128)S(1)}, u32[]{:S(2)}) copy-start(f32[768,512,4]{1,0,2:T(8,128)S(1)} %get-tuple-element.587) | copy-start | bytes 18874372 | tf_op jit(solution)/shard_map/while
  312.6 10.9 %copy-start.6 = (f32[3072,128]{1,0:T(8,128)S(1)}, f32[3072,128]{1,0:T(8,128)}, u32[]{:S(2)}) copy-start(f32[3072,128]{1,0:T(8,128)} %gather_fusion.3) | copy-start | bytes 4718596
  312.6 10.9 %copy-start.9 = (pred[16,192]{1,0:T(8,128)(4,1)S(1)}, pred[16,192]{1,0:T(8,128)(4,1)}, u32[]{:S(2)}) copy-start(pred[16,192]{1,0:T(8,128)(4,1)} %broadcast_in_dim.168) | copy-start | bytes 9220
  352.8 40.7 %all-to-all-start.7 = ((f32[16,192,128]{2,1,0:T(8,128)}), f32[16,192,128]{2,1,0:T(8,128)}, u32[]{:S(2)}, u32[]{:S(2)}) async-start(f32[16,192,128]{2,1,0:T(8,128)} %get-tuple-element.480), calls=%async_computation.7 | async-start | bytes 3145728 | tf_op jit(solution)/shard_map/all_to_all | solution.py:177
  360.6 15.4 %copy-start.3 = (bf16[2048,512]{1,0:T(8,128)(2,1)S(1)}, bf16[2048,512]{1,0:T(8,128)(2,1)}, u32[]{:S(2)}) copy-start(bf16[2048,512]{1,0:T(8,128)(2,1)} %get-tuple-element.378) | copy-start | bytes 6291460
  435.1 42.9 %all-to-all-start.5 = ((bf16[16,192,512]{2,1,0:T(8,128)(2,1)}), bf16[16,192,512]{2,1,0:T(8,128)(2,1)S(1)}, u32[]{:S(2)}, u32[]{:S(2)}) async-start(bf16[16,192,512]{2,1,0:T(8,128)(2,1)} %get-tuple-element.482), calls=%async_computation.5 | async-start | bytes 6291456 | tf_op jit(solution)/shard_map/all_to_all | solution.py:173
  442.5 4.9 %copy-start.5 = (bf16[16,192,512]{2,1,0:T(8,128)(2,1)S(1)}, bf16[16,192,512]{2,1,0:T(8,128)(2,1)}, u32[]{:S(2)}) copy-start(bf16[16,192,512]{2,1,0:T(8,128)(2,1)} %all_to_all.123) | copy-start | bytes 9437188
  478.0 2.1 copy-start.1
  (1 other events, 1.7 us)
where the time goes:
time: 488 us; the launch traced here: 480 us
  local copies, waits for them, and re-layouts  175 us (36%)
  matrix products  96.2 us (20%)
  blocking collectives  68.3 us (14%)
  waiting for transfers between devices  64.4 us (13%)
  starting transfers between devices  45.4 us (9%)
  other arithmetic  29.3 us (6%)
    gather x4, local copies, waits for them, and re-layouts, to_slots(): rows[safe_source]  50.6 us
    all_to_all x1, blocking collectives, local(): lax.all_to_all(to_slots(out_rows), 'seq', split_axis=0, concat_axis=1, ti...  41.6 us
    all_to_all x1, waiting for transfers between devices, local(): lax.all_to_all(to_slots(qgrad_rows), 'seq', split_axis=0, concat_axis=1,...  28.6 us
    all_to_all x1, blocking collectives, local(): lax.all_to_all(to_slots(kgrad_rows), 'seq', split_axis=0, concat_axis=1,...  26.7 us
    dot_general x4, matrix products, attend(): jnp.einsum('kprw,rkpd->wkd', prob_half, grad_block, preferred_element_typ...  23.2 us
    dot_general x4, matrix products, attend(): jnp.einsum('kprw,wkd->rkpd', prob_half, value_block, preferred_element_ty...  22.8 us
    all_to_all x1, waiting for transfers between devices, local(): lax.all_to_all(query_states, 'seq', split_axis=1, concat_axis=0, tiled=True)  19.7 us
    dynamic_update_slice x8, local copies, waits for them, and re-layouts, step(): lax.dynamic_update_slice_in_dim(qgrad_acc, qgrad_block.reshape(qblock, he...  17.1 us
  transfers between devices with their start and end apart: 6, of which 5 were waited for; matrix products, arithmetic and copies ran while one was open for 14% of the time, Pallas kernels for 0%

commit v1 on v0

v1 whole, which is shorter than its diff:
```python
import functools

import jax
import jax.numpy as jnp
from jax import lax
from jax.experimental import pallas as pl
from jax.experimental.pallas import tpu as pltpu
from jax.sharding import PartitionSpec as P

HEADS = 64
KV_HEADS = 8
HEAD_DIM = 128
BLOCK = 128
CAP = 192
HALO = 32
TOK = 128
WIN = TOK + 2 * HALO
GROUP = HEADS // KV_HEADS
GCOLS = GROUP * HEAD_DIM
QB = 64
NB = WIN // QB
CHUNK_HEADS = 4
CW = CHUNK_HEADS * QB
TALL = CAP + 2 * HALO
INV_ROOT = HEAD_DIM**-0.5
LOG2E = 1.4426950408889634
FAR = -1e30
EARLY = 0
MESH = pl.DeviceIdType.MESH
BF16 = jnp.bfloat16
F32 = jnp.float32


def dot(a, b, dims):
    return lax.dot_general(a, b, (dims, ((), ())), preferred_element_type=F32)


def clear(tall_refs):
    for ref in tall_refs:
        tail = ref.shape[:-2] + (TALL - WIN, HEAD_DIM)
        ref[..., WIN:TALL, :] = jnp.zeros(tail, F32)


def prepare(me, devices, len_ref, own_ref, table_ref, bias, owned, tall_refs):
    docs = len_ref.shape[0]
    base = me * TOK - HALO
    key_pos = base + lax.broadcasted_iota(jnp.int32, (WIN, 128), 0)
    lane = lax.broadcasted_iota(jnp.int32, (8, CW), 1) % QB
    query_pos = [base + b * QB + lane for b in range(NB)]

    def one(n, carry):
        start, first, count, key_doc, query_doc = carry
        length = len_ref[n]
        owner = own_ref[n]
        key_doc = key_doc + jnp.where(key_pos >= start, 1, 0)
        query_doc = tuple(
            d + jnp.where(p >= start, 1, 0) for d, p in zip(query_doc, query_pos)
        )
        first = first + jnp.where(owner < me, length, 0)
        count = count + jnp.where(owner == me, length, 0)
        return (start + length, first, count, key_doc, query_doc)

    zero = jnp.int32(0)
    _, first, count, key_doc, query_doc = lax.fori_loop(
        0,
        docs,
        one,
        (
            zero,
            zero,
            zero,
            jnp.zeros((WIN, 128), jnp.int32),
            tuple(jnp.zeros((8, CW), jnp.int32) for _ in range(NB)),
        ),
    )
    before = jnp.maximum(me - 1, 0)
    after = jnp.minimum(me + 1, devices - 1)
    own_before = table_ref[me, before]
    after_own = table_ref[after, me]
    after_before = table_ref[after, before]
    key_pos2 = jnp.concatenate([key_pos] * (CW // 128), axis=1)
    key_doc2 = jnp.concatenate([key_doc] * (CW // 128), axis=1)
    for b in range(NB):
        rows = (b + 1) * QB
        kp, kd = key_pos2[:rows], key_doc2[:rows]
        qp, qd = query_pos[b][:1], query_doc[b][:1]
        key_block = (kp + BLOCK) // BLOCK - me
        query_block = (qp + BLOCK) // BLOCK - me
        linked = jnp.where(
            query_block == 1,
            jnp.where(key_block == 0, own_before, 1),
            jnp.where(
                query_block == 2,
                jnp.where(key_block == 0, after_before, jnp.where(key_block == 1, after_own, 1)),
                1,
            ),
        )
        allowed = (kd == qd) & (kp <= qp) & (linked == 1)
        bias[b, 0:rows, :] = jnp.where(allowed, 0.0, FAR)
        inside = (query_pos[b] >= first) & (query_pos[b] < first + count)
        owned[b] = jnp.where(inside, 1.0, 0.0)
    clear(tall_refs)
    return first - base


def group_pass(q, g, k, v, bias, owned, out_tall, dq_tall, dk_tall, dv_tall):
    for b in reversed(range(NB)):
        rows = (b + 1) * QB
        keys, values = k[0:rows, :], v[0:rows, :]
        dk = dv = None
        for c in range(GROUP // CHUNK_HEADS):
            heads = range(c * CHUNK_HEADS, (c + 1) * CHUNK_HEADS)
            span = slice(b * QB, (b + 1) * QB)
            qs = jnp.concatenate([q[span, h * HEAD_DIM : (h + 1) * HEAD_DIM] for h in heads], axis=0)
            gs = jnp.concatenate([g[span, h * HEAD_DIM : (h + 1) * HEAD_DIM] for h in heads], axis=0)
            scores = dot(keys, qs, ((1,), (1,))) * (INV_ROOT * LOG2E) + bias[b, 0:rows, :]
            highest = jnp.max(scores, axis=0, keepdims=True)
            raised = jnp.exp2(scores - highest)
            total = jnp.sum(raised, axis=0, keepdims=True)
            prob = raised * (owned[b, 0:1, :] / total)
            half = prob.astype(BF16)
            prob_grad = dot(values, gs, ((1,), (1,)))
            delta = jnp.sum(prob * prob_grad, axis=0, keepdims=True)
            score_grad = (prob * (prob_grad - delta)).astype(BF16)
            out = dot(half, values, ((0,), (0,)))
            dq = dot(score_grad, keys, ((0,), (0,))) * INV_ROOT
            for i, h in enumerate(heads):
                out_tall[h, span, :] = out[i * QB : (i + 1) * QB]
                dq_tall[h, span, :] = dq[i * QB : (i + 1) * QB]
            dk_part = dot(score_grad, qs, ((1,), (0,)))
            dv_part = dot(half, gs, ((1,), (0,)))
            dk = dk_part if dk is None else dk + dk_part
            dv = dv_part if dv is None else dv + dv_part
        if b == NB - 1:
            dk_tall[0:rows, :] = dk
            dv_tall[0:rows, :] = dv
        else:
            dk_tall[0:rows, :] += dk
            dv_tall[0:rows, :] += dv


def shifted(shift, out_tall, dq_tall, dk_tall, dv_tall, out, dq, dk, dv):
    rows = pl.ds(shift, CAP)
    for h in range(GROUP):
        cols = slice(h * HEAD_DIM, (h + 1) * HEAD_DIM)
        out[:, cols] = out_tall[h, rows, :].astype(BF16)
        dq[:, cols] = dq_tall[h, rows, :].astype(BF16)
    dk[...] = (dk_tall[rows, :] * INV_ROOT).astype(BF16)
    dv[...] = dv_tall[rows, :].astype(BF16)


def windows(groups):
    return [(groups, WIN, GCOLS)] * 2 + [(groups, WIN, HEAD_DIM)] * 2


def tall_scratch():
    return [
        pltpu.VMEM((GROUP, TALL, HEAD_DIM), F32),
        pltpu.VMEM((GROUP, TALL, HEAD_DIM), F32),
        pltpu.VMEM((TALL, HEAD_DIM), F32),
        pltpu.VMEM((TALL, HEAD_DIM), F32),
    ]


def wide(g):
    return pl.ds(pl.multiple_of(g * GCOLS, GCOLS), GCOLS)


def thin(g):
    return pl.ds(pl.multiple_of(g * HEAD_DIM, HEAD_DIM), HEAD_DIM)


COLUMNS = (wide, wide, thin, thin)


def exchange_kernel(devices, early, *refs):
    q, g, k, v, lens, owners, table = refs[:7]
    late_windows = refs[7:11]
    bias, owned = refs[11:13]
    rest = refs[13:-3]
    done, near = (rest[:4], rest[4:8]) if early else ((), ())
    talls = rest[-4:]
    send, recv, load = refs[-3:]
    dp = lax.axis_index("dp")
    me = lax.axis_index("seq")
    right, left = lax.rem(me + 1, devices), lax.rem(me + devices - 1, devices)
    sources = (q, g, k, v)

    def window(n, a):
        if isinstance(n, int) and n >= early:
            return late_windows[a].at[n - early]
        return near[a].at[n]

    def hop(n, a, side):
        rows = pl.ds(TOK - HALO, HALO) if side == 0 else pl.ds(0, HALO)
        there = pl.ds(0, HALO) if side == 0 else pl.ds(HALO + TOK, HALO)
        return pltpu.make_async_remote_copy(
            src_ref=sources[a].at[rows, COLUMNS[a](n)],
            dst_ref=window(n, a).at[there, :],
            send_sem=send.at[n, a, side],
            recv_sem=recv.at[n, a, side],
            device_id=(dp, right if side == 0 else left),
            device_id_type=MESH,
        )

    def own(n, a):
        return pltpu.make_async_copy(
            sources[a].at[:, COLUMNS[a](n)], window(n, a).at[pl.ds(HALO, TOK), :], load.at[n, a]
        )

    barrier = pltpu.get_barrier_semaphore()
    for neighbour in (left, right):
        pl.semaphore_signal(barrier, inc=1, device_id=(dp, neighbour), device_id_type=MESH)
    pl.semaphore_wait(barrier, 2)
    for n in range(KV_HEADS):
        for a in (2, 3, 0, 1):
            for side in range(2):
                hop(n, a, side).start()
    for n in range(KV_HEADS):
        for a in range(4):
            own(n, a).start()
    shift = prepare(me, devices, lens, owners, table, bias, owned, talls)

    def step(n, carry):
        for a in range(4):
            own(n, a).wait()
            for side in range(2):
                hop(n, a, side).wait()
        group_pass(*(w.at[n] for w in near), bias, owned, *talls)
        shifted(shift, *talls, *(d.at[n] for d in done))
        return carry

    if early:
        lax.fori_loop(0, early, step, 0)
    for n in range(early, KV_HEADS):
        for a in range(4):
            own(n, a).wait()
            for side in range(2):
                hop(n, a, side).wait()


def finish_kernel(early, *refs):
    late = KV_HEADS - early
    lens, owners = refs[:2]
    late_windows = refs[2:6]
    bias, owned = refs[6:8]
    done = refs[8:-13]
    outs = refs[-13:-9]
    stage = refs[-9:-5]
    talls = refs[-5:-1]
    store = refs[-1]
    me = lax.axis_index("seq")

    def write(n, a):
        src = done[a].at[n] if n < early else stage[a].at[n - early]
        return pltpu.make_async_copy(src, outs[a].at[:, COLUMNS[a](n)], store.at[n, a])

    for n in range(early):
        for a in range(4):
            write(n, a).start()

    def one(n, first):
        return first + jnp.where(owners[n] < me, lens[n], 0)

    shift = lax.fori_loop(0, lens.shape[0], one, jnp.int32(0)) - (me * TOK - HALO)
    clear(talls)
    for n in range(late):
        group_pass(*(w.at[n] for w in late_windows), bias, owned, *talls)
        shifted(shift, *talls, *(s.at[n] for s in stage))
        for a in range(4):
            write(early + n, a).start()
    for n in range(KV_HEADS):
        for a in range(4):
            write(n, a).wait()


def local(devices, early, q, k, v, g, lens, owners, table):
    late = KV_HEADS - early
    any_spec = pl.BlockSpec(memory_space=pl.ANY)
    smem = pl.BlockSpec(memory_space=pltpu.SMEM)
    arrays = [pltpu.with_memory_space_constraint(x, pltpu.HBM) for x in (q, g, k, v)]
    lens, owners, table = [pltpu.with_memory_space_constraint(x, pltpu.HBM) for x in (lens, owners, table)]
    results = [(CAP, GCOLS)] * 2 + [(CAP, HEAD_DIM)] * 2
    mid_shapes = (
        [pltpu.VMEM(s, BF16) for s in windows(late)]
        + [pltpu.VMEM((NB, WIN, CW), F32), pltpu.VMEM((NB, 8, CW), F32)]
        + [pltpu.VMEM((early, *s), BF16) for s in results if early]
    )
    mid = pl.pallas_call(
        functools.partial(exchange_kernel, devices, early),
        out_shape=mid_shapes,
        in_specs=[any_spec] * 4 + [smem] * 3,
        out_specs=[pl.BlockSpec(memory_space=pltpu.VMEM)] * len(mid_shapes),
        scratch_shapes=[pltpu.VMEM(s, BF16) for s in windows(early) if early]
        + tall_scratch()
        + [
            pltpu.SemaphoreType.DMA((KV_HEADS, 4, 2)),
            pltpu.SemaphoreType.DMA((KV_HEADS, 4, 2)),
            pltpu.SemaphoreType.DMA((KV_HEADS, 4)),
        ],
        compiler_params=pltpu.CompilerParams(
            collective_id=0, has_side_effects=True, vmem_limit_bytes=24 << 20
        ),
        name="exchange",
    )(*arrays, lens, owners, table)
    mid = [pltpu.with_memory_space_constraint(x, pltpu.VMEM) for x in mid]
    shapes = [(CAP, w) for w in (HEADS * HEAD_DIM,) * 2 + (KV_HEADS * HEAD_DIM,) * 2]
    return tuple(
        pl.pallas_call(
            functools.partial(finish_kernel, early),
            out_shape=[pltpu.HBM(s, BF16) for s in shapes],
            in_specs=[smem] * 2 + [pl.BlockSpec(memory_space=pltpu.VMEM)] * len(mid),
            out_specs=[any_spec] * 4,
            scratch_shapes=[pltpu.VMEM((late, *s), BF16) for s in results]
            + tall_scratch()
            + [pltpu.SemaphoreType.DMA((KV_HEADS, 4))],
            compiler_params=pltpu.CompilerParams(vmem_limit_bytes=24 << 20),
            name="finish",
        )(lens, owners, *mid)
    )


def solution(mesh):
    rows = P(("dp", "seq"), None)
    return jax.shard_map(
        functools.partial(local, mesh.shape["seq"], EARLY),
        mesh=mesh,
        in_specs=(rows, rows, rows, rows, P("dp"), P("dp"), P("dp", None)),
        out_specs=(rows, rows, rows, rows),
        check_vma=False,
    )
```

time: 488 us -> 56.4 us (0.12)
  the two profiles are of different devices: /device:TPU:174 before, /device:TPU:192 now
where the time goes in v1:
time: 56.4 us; the launch traced here: 56.2 us
  Pallas kernels  55.6 us (99%)
  between operations  0.64 us (1%)
    pallas_call x1, Pallas kernels, local(): pl.pallas_call(functools.partial(exchange_kernel, devices, early), out_sh...  34.4 us
    pallas_call x1, Pallas kernels, local(): pl.pallas_call(functools.partial(finish_kernel, early), out_shape=[pltpu....  21.2 us

profile of v1, /device:TPU:192, one launch (start us, length us, event | category | flops | bytes accessed | tf_op | source)
XLA Modules:
  0.0 56.2 jit_solution(6674354819394938748)
XLA Ops:
  0.6 34.4 %exchange.1 = (bf16[8,192,1024]{2,1,0:T(8,128)(2,1)S(1)}, bf16[8,192,1024]{2,1,0:T(8,128)(2,1)S(1)}, bf16[8,192,128]{2,1,0:T(8,128)(2,1)S(1)}, bf16[8,192,128]{2...) custom-call(bf16[128,8192]{1,0:T(8,128)(2,1)} %refs_0_.2, bf16[128,8192]{1,0:T(8,128)(2,1)} %refs_1_.2, ...), custom_call_target="tpu_custom_call" | custom-call | tf_op jit(solution)/shard_map/exchange/pallas_call | solution.py:289
  35.0 21.2 %finish.1 = (bf16[192,8192]{1,0:T(8,128)(2,1)}, bf16[192,8192]{1,0:T(8,128)(2,1)}, bf16[192,1024]{1,0:T(8,128)(2,1)}, bf16[192,1024]{1,0:T(8,128)(2,1)}) custom-call(s32[32]{0:T(128)} %refs_0_.3, s32[32]{0:T(128)} %refs_1_.3, bf16[8,192,1024]{2,1,0:T(8,128)(2,1)S(1)} %get-tuple-element.10.refs_2_, bf16[8,192,1024]{2,1,0:T(8,128)(2,1)S(1)} %get-tuple-element.11.refs_3_, ...), custom_call_target="tpu_custom_call" | custom-call | tf_op jit(solution)/shard_map/finish/pallas_call | solution.py:309

commit v2 on v1

--- a/solution.py
+++ b/solution.py
@@ -25,7 +25,7 @@
 INV_ROOT = HEAD_DIM**-0.5
 LOG2E = 1.4426950408889634
 FAR = -1e30
-EARLY = 0
+EARLY = 7
 MESH = pl.DeviceIdType.MESH
 BF16 = jnp.bfloat16
 F32 = jnp.float32
@@ -100,7 +100,7 @@
         inside = (query_pos[b] >= first) & (query_pos[b] < first + count)
         owned[b] = jnp.where(inside, 1.0, 0.0)
     clear(tall_refs)
-    return first - base
+    return jnp.clip(first - base, 0, 2 * HALO)
 
 
 def group_pass(q, g, k, v, bias, owned, out_tall, dq_tall, dk_tall, dv_tall):
@@ -177,9 +177,9 @@
     q, g, k, v, lens, owners, table = refs[:7]
     late_windows = refs[7:11]
     bias, owned = refs[11:13]
-    rest = refs[13:-3]
-    done, near = (rest[:4], rest[4:8]) if early else ((), ())
-    talls = rest[-4:]
+    done = refs[13:17]
+    near = [refs[17 + 4 * n : 21 + 4 * n] for n in range(early)]
+    talls = refs[-7:-3]
     send, recv, load = refs[-3:]
     dp = lax.axis_index("dp")
     me = lax.axis_index("seq")
@@ -187,9 +187,7 @@
     sources = (q, g, k, v)
 
     def window(n, a):
-        if isinstance(n, int) and n >= early:
-            return late_windows[a].at[n - early]
-        return near[a].at[n]
+        return near[n][a] if n < early else late_windows[a].at[n - early]
 
     def hop(n, a, side):
         rows = pl.ds(TOK - HALO, HALO) if side == 0 else pl.ds(0, HALO)
@@ -221,22 +219,14 @@
             own(n, a).start()
     shift = prepare(me, devices, lens, owners, table, bias, owned, talls)
 
-    def step(n, carry):
+    for n in range(KV_HEADS):
         for a in range(4):
             own(n, a).wait()
             for side in range(2):
                 hop(n, a, side).wait()
-        group_pass(*(w.at[n] for w in near), bias, owned, *talls)
-        shifted(shift, *talls, *(d.at[n] for d in done))
-        return carry
-
-    if early:
-        lax.fori_loop(0, early, step, 0)
-    for n in range(early, KV_HEADS):
-        for a in range(4):
-            own(n, a).wait()
-            for side in range(2):
-                hop(n, a, side).wait()
+        if n < early:
+            group_pass(*near[n], bias, owned, *talls)
+            shifted(shift, *talls, *(d.at[n] for d in done))
 
 
 def finish_kernel(early, *refs):
@@ -244,11 +234,11 @@
     lens, owners = refs[:2]
     late_windows = refs[2:6]
     bias, owned = refs[6:8]
-    done = refs[8:-13]
-    outs = refs[-13:-9]
-    stage = refs[-9:-5]
-    talls = refs[-5:-1]
-    store = refs[-1]
+    done = refs[8:12]
+    outs = refs[12:16]
+    stage = refs[16:20]
+    talls = refs[20:24]
+    store = refs[24]
     me = lax.axis_index("seq")
 
     def write(n, a):
@@ -263,6 +253,7 @@
         return first + jnp.where(owners[n] < me, lens[n], 0)
 
     shift = lax.fori_loop(0, lens.shape[0], one, jnp.int32(0)) - (me * TOK - HALO)
+    shift = jnp.clip(shift, 0, 2 * HALO)
     clear(talls)
     for n in range(late):
         group_pass(*(w.at[n] for w in late_windows), bias, owned, *talls)
@@ -284,14 +275,14 @@
     mid_shapes = (
         [pltpu.VMEM(s, BF16) for s in windows(late)]
         + [pltpu.VMEM((NB, WIN, CW), F32), pltpu.VMEM((NB, 8, CW), F32)]
-        + [pltpu.VMEM((early, *s), BF16) for s in results if early]
+        + [pltpu.VMEM((early, *s), BF16) for s in results]
     )
     mid = pl.pallas_call(
         functools.partial(exchange_kernel, devices, early),
         out_shape=mid_shapes,
         in_specs=[any_spec] * 4 + [smem] * 3,
         out_specs=[pl.BlockSpec(memory_space=pltpu.VMEM)] * len(mid_shapes),
-        scratch_shapes=[pltpu.VMEM(s, BF16) for s in windows(early) if early]
+        scratch_shapes=[pltpu.VMEM(s[1:], BF16) for s in windows(1) * early]
         + tall_scratch()
         + [
             pltpu.SemaphoreType.DMA((KV_HEADS, 4, 2)),

time: 56.4 us -> 40.6 us (0.72)
  the two profiles are of different devices: /device:TPU:192 before, /device:TPU:32 now
where the time goes in v2:
time: 40.6 us; the launch traced here: 40.4 us
  Pallas kernels  39.6 us (98%)
  between operations  0.8 us (2%)
    pallas_call x1, Pallas kernels, local(): pl.pallas_call(functools.partial(exchange_kernel, devices, early), out_sh...  35.1 us
    pallas_call x1, Pallas kernels, local(): pl.pallas_call(functools.partial(finish_kernel, early), out_shape=[pltpu....  4.53 us

profile of v2, /device:TPU:32, one launch (start us, length us, event | category | flops | bytes accessed | tf_op | source)
XLA Modules:
  0.0 40.4 jit_solution(6402963541771042264)
XLA Ops:
  0.6 35.1 %exchange.1 = (bf16[1,192,1024]{2,1,0:T(8,128)(2,1)S(1)}, bf16[1,192,1024]{2,1,0:T(8,128)(2,1)S(1)}, bf16[1,192,128]{2,1,0:T(8,128)(2,1)S(1)}, bf16[1,192,128]{2...) custom-call(bf16[128,8192]{1,0:T(8,128)(2,1)} %refs_0_.2, ...), custom_call_target="tpu_custom_call" | custom-call | tf_op jit(solution)/shard_map/exchange/pallas_call | solution.py:280
  35.7 4.5 %finish.1 = (bf16[192,8192]{1,0:T(8,128)(2,1)}, bf16[192,8192]{1,0:T(8,128)(2,1)}, bf16[192,1024]{1,0:T(8,128)(2,1)}, bf16[192,1024]{1,0:T(8,128)(2,1)}) custom-call(s32[32]{0:T(128)} %refs_0_.3, s32[32]{0:T(128)} %refs_1_.3, bf16[1,192,1024]{2,1,0:T(8,128)(2,1)S(1)} %get-tuple-element.14.refs_2_, bf16[1,192,1024]{2,1,0:T(8,128)(2,1)S(1)} %get-tuple-element.15.refs_3_, ...), custom_call_target="tpu_custom_call" | custom-call | tf_op jit(solution)/shard_map/finish/pallas_call | solution.py:300

commit v3 on v2

v3 whole, which is shorter than its diff:
```python
import functools

import jax
import jax.numpy as jnp
from jax import lax
from jax.experimental import pallas as pl
from jax.experimental.pallas import tpu as pltpu
from jax.sharding import PartitionSpec as P

HEADS = 64
KV_HEADS = 8
HEAD_DIM = 128
BLOCK = 128
CAP = 192
HALO = 32
TOK = 128
WIN = TOK + 2 * HALO
GROUP = HEADS // KV_HEADS
GCOLS = GROUP * HEAD_DIM
QB = 64
CHUNK_HEADS = 4
CW = CHUNK_HEADS * QB
OWN_BLOCKS = ((HALO + QB, QB, HALO + 2 * QB), (HALO, QB, HALO + QB))
HALO_BLOCKS = ((HALO + TOK, HALO, WIN), (0, HALO, HALO))
BLOCKS = OWN_BLOCKS + HALO_BLOCKS
TALL = CAP + 2 * HALO
INV_ROOT = HEAD_DIM**-0.5
LOG2E = 1.4426950408889634
FAR = -1e30
MESH = pl.DeviceIdType.MESH
BF16 = jnp.bfloat16
F32 = jnp.float32


def dot(a, b, dims):
    return lax.dot_general(a, b, (dims, ((), ())), preferred_element_type=F32)


def clear(tall_refs):
    for ref in tall_refs:
        tail = ref.shape[:-2] + (TALL - WIN, HEAD_DIM)
        ref[..., WIN:TALL, :] = jnp.zeros(tail, F32)


def prepare(me, devices, len_ref, own_ref, table_ref, biases, owned):
    docs = len_ref.shape[0]
    base = me * TOK - HALO
    key_pos = base + lax.broadcasted_iota(jnp.int32, (WIN, 128), 0)
    lane = lax.broadcasted_iota(jnp.int32, (8, CW), 1)
    query_pos = [base + first + lane % count for first, count, _ in BLOCKS]

    def one(n, carry):
        start, first, count, key_doc, query_doc = carry
        length = len_ref[n]
        owner = own_ref[n]
        key_doc = key_doc + jnp.where(key_pos >= start, 1, 0)
        query_doc = tuple(
            d + jnp.where(p >= start, 1, 0) for d, p in zip(query_doc, query_pos)
        )
        first = first + jnp.where(owner < me, length, 0)
        count = count + jnp.where(owner == me, length, 0)
        return (start + length, first, count, key_doc, query_doc)

    zero = jnp.int32(0)
    _, first, count, key_doc, query_doc = lax.fori_loop(
        0,
        docs,
        one,
        (
            zero,
            zero,
            zero,
            jnp.zeros((WIN, 128), jnp.int32),
            tuple(jnp.zeros((8, CW), jnp.int32) for _ in BLOCKS),
        ),
    )
    before = jnp.maximum(me - 1, 0)
    after = jnp.minimum(me + 1, devices - 1)
    own_before = table_ref[me, before]
    after_own = table_ref[after, me]
    after_before = table_ref[after, before]
    key_pos2 = jnp.concatenate([key_pos] * (CW // 128), axis=1)
    key_doc2 = jnp.concatenate([key_doc] * (CW // 128), axis=1)
    for b, (_, _, rows) in enumerate(BLOCKS):
        kp, kd = key_pos2[:rows], key_doc2[:rows]
        qp, qd = query_pos[b][:1], query_doc[b][:1]
        key_block = (kp + BLOCK) // BLOCK - me
        query_block = (qp + BLOCK) // BLOCK - me
        linked = jnp.where(
            query_block == 1,
            jnp.where(key_block == 0, own_before, 1),
            jnp.where(
                query_block == 2,
                jnp.where(key_block == 0, after_before, jnp.where(key_block == 1, after_own, 1)),
                1,
            ),
        )
        allowed = (kd == qd) & (kp <= qp) & (linked == 1)
        biases[b][...] = jnp.where(allowed, 0.0, FAR)
        inside = (query_pos[b] >= first) & (query_pos[b] < first + count)
        owned[b] = jnp.where(inside, 1.0, 0.0)
    return jnp.clip(first - base, 0, 2 * HALO)


def block_pass(b, heads, q, g, k, v, bias, owned, out_tall, dq_tall):
    first, count, rows = BLOCKS[b]
    span = slice(first, first + count)
    width = count * len(heads)
    keys, values = k[0:rows, :], v[0:rows, :]
    qs = jnp.concatenate([q[span, h * HEAD_DIM : (h + 1) * HEAD_DIM] for h in heads], axis=0)
    gs = jnp.concatenate([g[span, h * HEAD_DIM : (h + 1) * HEAD_DIM] for h in heads], axis=0)
    scores = dot(keys, qs, ((1,), (1,))) * (INV_ROOT * LOG2E) + bias[:, 0:width]
    highest = jnp.max(scores, axis=0, keepdims=True)
    raised = jnp.exp2(scores - highest)
    total = jnp.sum(raised, axis=0, keepdims=True)
    prob = raised * (owned[b, 0:1, 0:width] / total)
    half = prob.astype(BF16)
    prob_grad = dot(values, gs, ((1,), (1,)))
    delta = jnp.sum(prob * prob_grad, axis=0, keepdims=True)
    score_grad = (prob * (prob_grad - delta)).astype(BF16)
    out = dot(half, values, ((0,), (0,)))
    dq = dot(score_grad, keys, ((0,), (0,))) * INV_ROOT
    for i, h in enumerate(heads):
        out_tall[h, span, :] = out[i * count : (i + 1) * count]
        dq_tall[h, span, :] = dq[i * count : (i + 1) * count]
    return dot(score_grad, qs, ((1,), (0,))), dot(half, gs, ((1,), (0,)))


def own_pass(fresh, q, g, k, v, biases, owned, out_tall, dq_tall, dk_tall, dv_tall):
    count = q.shape[1] // HEAD_DIM
    for b, (_, _, rows) in enumerate(OWN_BLOCKS):
        dk = dv = None
        for c in range(count // CHUNK_HEADS):
            heads = range(c * CHUNK_HEADS, (c + 1) * CHUNK_HEADS)
            dk_part, dv_part = block_pass(b, heads, q, g, k, v, biases[b], owned, out_tall, dq_tall)
            dk = dk_part if dk is None else dk + dk_part
            dv = dv_part if dv is None else dv + dv_part
        if fresh and b == 0:
            dk_tall[0:rows, :] = dk
            dv_tall[0:rows, :] = dv
        else:
            dk_tall[0:rows, :] += dk
            dv_tall[0:rows, :] += dv


def halo_pass(fresh, q, g, k, v, biases, owned, out_tall, dq_tall, dk_tall, dv_tall):
    heads = range(q.shape[1] // HEAD_DIM)
    for b, (_, _, rows) in enumerate(BLOCKS):
        if b < len(OWN_BLOCKS):
            continue
        dk, dv = block_pass(b, heads, q, g, k, v, biases[b], owned, out_tall, dq_tall)
        old = min(rows, HALO + TOK) if fresh else rows
        dk_tall[0:old, :] += dk[0:old]
        dv_tall[0:old, :] += dv[0:old]
        if old < rows:
            dk_tall[old:rows, :] = dk[old:rows]
            dv_tall[old:rows, :] = dv[old:rows]


def shift_queries(shift, out_tall, dq_tall, out, dq):
    rows = pl.ds(shift, CAP)
    for h in range(out.shape[1] // HEAD_DIM):
        cols = slice(h * HEAD_DIM, (h + 1) * HEAD_DIM)
        out[:, cols] = out_tall[h, rows, :].astype(BF16)
        dq[:, cols] = dq_tall[h, rows, :].astype(BF16)


def shift_keys(shift, dk_tall, dv_tall, dk, dv):
    rows = pl.ds(shift, CAP)
    dk[...] = (dk_tall[rows, :] * INV_ROOT).astype(BF16)
    dv[...] = dv_tall[rows, :].astype(BF16)


AHEAD = 2
UNITS = [(n, 0, GROUP) for n in range(KV_HEADS - 1)] + [
    (KV_HEADS - 1, 0, GROUP // 2),
    (KV_HEADS - 1, GROUP // 2, GROUP // 2),
]
LAST_COLS = UNITS[-1][2] * HEAD_DIM
EARLY_COLS = HEADS * HEAD_DIM - LAST_COLS
KV_COLS = KV_HEADS * HEAD_DIM
EARLY_KV = KV_COLS - HEAD_DIM


def unit_cols(u):
    n, first, count = UNITS[u]
    return pl.ds(n * GCOLS + first * HEAD_DIM, count * HEAD_DIM)


def kv_cols(n):
    return pl.ds(n * HEAD_DIM, HEAD_DIM)


def exchange_kernel(devices, *refs):
    q, g, k, v, lens, owners, table = refs[:7]
    kw, vw = refs[7:9]
    halo_biases = refs[9:11]
    owned, last_q, last_g, done_o, done_q, done_k, done_v = refs[11:18]
    last_talls, last_kv_talls = refs[18:20], refs[20:22]
    biases = refs[22:24] + halo_biases
    early = len(UNITS) - 1
    at = 24
    near = [refs[at + 2 * u : at + 2 + 2 * u] for u in range(early)] + [(last_q, last_g)]
    at += 2 * early
    talls = [refs[at + 2 * u : at + 2 + 2 * u] for u in range(early)] + [last_talls]
    at += 2 * early
    kv_talls = [refs[at + 2 * n : at + 2 + 2 * n] for n in range(KV_HEADS - 1)] + [last_kv_talls]
    send, recv, load, kv_send, kv_recv, kv_load = refs[-6:]
    dp = lax.axis_index("dp")
    me = lax.axis_index("seq")
    has = (me < devices - 1, me > 0)
    peer = (jnp.minimum(me + 1, devices - 1), jnp.maximum(me - 1, 0))

    def hop(src, cols, dst, side, sems):
        rows = pl.ds(TOK - HALO, HALO) if side == 0 else pl.ds(0, HALO)
        there = pl.ds(0, HALO) if side == 0 else pl.ds(HALO + TOK, HALO)
        return pltpu.make_async_remote_copy(
            src_ref=src.at[rows, cols],
            dst_ref=dst.at[there, :],
            send_sem=sems[0],
            recv_sem=sems[1],
            device_id=(dp, peer[side]),
            device_id_type=MESH,
        )

    def own(src, cols, dst, sem):
        return pltpu.make_async_copy(src.at[:, cols], dst.at[pl.ds(HALO, TOK), :], sem)

    every = pl.ds(0, KV_COLS)
    kv = ((k, kw), (v, vw))
    kv_hops = [
        [hop(src, every, dst, side, (kv_send.at[a, side], kv_recv.at[a, side])) for a, (src, dst) in enumerate(kv)]
        for side in range(2)
    ]
    kv_own = [own(src, every, dst, kv_load.at[a]) for a, (src, dst) in enumerate(kv)]
    hops = [
        [
            [
                hop(src, unit_cols(u), near[u][a], side, (send.at[u, a, side], recv.at[u, a, side]))
                for a, src in enumerate((q, g))
            ]
            for side in range(2)
        ]
        for u in range(len(UNITS))
    ]
    owns = [
        [own(src, unit_cols(u), near[u][a], load.at[u, a]) for a, src in enumerate((q, g))]
        for u in range(len(UNITS))
    ]

    barrier = pltpu.get_barrier_semaphore()
    for side in range(2):

        @pl.when(has[side])
        def _():
            pl.semaphore_signal(barrier, inc=1, device_id=(dp, peer[side]), device_id_type=MESH)

    peers = jnp.where(has[0], 1, 0) + jnp.where(has[1], 1, 0)
    pl.semaphore_wait(barrier, peers)
    for part in [kv_hops] + hops:
        for side in range(2):

            @pl.when(has[side])
            def _():
                for copy in part[side]:
                    copy.start()

    for part in [kv_own] + owns:
        for copy in part:
            copy.start()
    buffers = [ref for pair in near for ref in pair] + [kw, vw]
    for side in range(2):

        @pl.when(jnp.logical_not(has[1 - side]))
        def _():
            for ref in buffers:
                rows = pl.ds(0, HALO) if side == 0 else pl.ds(HALO + TOK, HALO)
                ref[rows, :] = jnp.zeros((HALO, ref.shape[1]), BF16)

    shift = prepare(me, devices, lens, owners, table, biases, owned)
    for pair in talls + kv_talls:
        clear(pair)

    def arrive(part):
        for side in range(2):

            @pl.when(has[side])
            def _():
                for copy in part[side]:
                    copy.wait_send()

            @pl.when(has[1 - side])
            def _():
                for copy in part[side]:
                    copy.wait_recv()

    def operands(u):
        n, first, count = UNITS[u]
        return (
            first == 0, *near[u], kw.at[:, kv_cols(n)], vw.at[:, kv_cols(n)], biases, owned,
            *talls[u], *kv_talls[n],
        )

    def own_rows(u):
        for copy in owns[u]:
            copy.wait()
        own_pass(*operands(u))

    for copy in kv_own:
        copy.wait()
    arrive(kv_hops)
    for u in range(AHEAD):
        own_rows(u)
    for u, (n, first, count) in enumerate(UNITS):
        if u + AHEAD < len(UNITS):
            own_rows(u + AHEAD)
        arrive(hops[u])
        if u == early:
            break
        halo_pass(*operands(u))
        shift_queries(shift, *talls[u], done_o.at[:, unit_cols(u)], done_q.at[:, unit_cols(u)])
        if first + count == GROUP:
            shift_keys(shift, *kv_talls[n], done_k.at[:, kv_cols(n)], done_v.at[:, kv_cols(n)])


def finish_kernel(lens, owners, kw, vw, bias_after, bias_before, owned, last_q, last_g, done_o, done_q, done_k, done_v,
                  out_part, dq_part, dk_part, dv_part, out, dq, dk, dv, stage_o, stage_q, stage_k, stage_v,
                  out_tall, dq_tall, dk_tall, dv_tall, flush, store):
    me = lax.axis_index("seq")
    pieces = 4
    width = EARLY_COLS // pieces
    moves = []
    for p in range(pieces):
        cols = pl.ds(p * width, width)
        moves.append(pltpu.make_async_copy(done_o.at[:, cols], out.at[:, cols], flush.at[p, 0]))
        moves.append(pltpu.make_async_copy(done_q.at[:, cols], dq.at[:, cols], flush.at[p, 1]))
    cols = pl.ds(0, EARLY_KV)
    moves.append(pltpu.make_async_copy(done_k, dk.at[:, cols], flush.at[pieces, 0]))
    moves.append(pltpu.make_async_copy(done_v, dv.at[:, cols], flush.at[pieces, 1]))
    for move in moves:
        move.start()

    def one(n, first):
        return first + jnp.where(owners[n] < me, lens[n], 0)

    shift = lax.fori_loop(0, lens.shape[0], one, jnp.int32(0)) - (me * TOK - HALO)
    shift = jnp.clip(shift, 0, 2 * HALO)
    middle = slice(HALO, HALO + TOK)
    for ref, part in ((out_tall, out_part), (dq_tall, dq_part)):
        ref[:, middle, :] = part[:, middle, :]
    clear((out_tall, dq_tall))
    dk_tall[...] = dk_part[...]
    dv_tall[...] = dv_part[...]
    n = KV_HEADS - 1
    halo_pass(
        False, last_q, last_g, kw.at[:, kv_cols(n)], vw.at[:, kv_cols(n)], (None, None, bias_after, bias_before), owned,
        out_tall, dq_tall, dk_tall, dv_tall,
    )
    shift_queries(shift, out_tall, dq_tall, stage_o, stage_q)
    shift_keys(shift, dk_tall, dv_tall, stage_k, stage_v)
    cols = pl.ds(EARLY_COLS, LAST_COLS)
    rest = [
        pltpu.make_async_copy(stage_o, out.at[:, cols], store.at[0]),
        pltpu.make_async_copy(stage_q, dq.at[:, cols], store.at[1]),
        pltpu.make_async_copy(stage_k, dk.at[:, kv_cols(n)], store.at[2]),
        pltpu.make_async_copy(stage_v, dv.at[:, kv_cols(n)], store.at[3]),
    ]
    for move in rest:
        move.start()
    for move in moves + rest:
        move.wait()


def local(devices, q, k, v, g, lens, owners, table):
    any_spec = pl.BlockSpec(memory_space=pl.ANY)
    vmem = pl.BlockSpec(memory_space=pltpu.VMEM)
    smem = pl.BlockSpec(memory_space=pltpu.SMEM)
    q, k, v, g, lens, owners, table = [
        pltpu.with_memory_space_constraint(x, pltpu.HBM) for x in (q, k, v, g, lens, owners, table)
    ]
    def tall(count):
        return pltpu.VMEM((count, TALL, HEAD_DIM), F32)

    def bias(b):
        return pltpu.VMEM((BLOCKS[b][2], CW), F32)

    kv_tall = pltpu.VMEM((TALL, HEAD_DIM), F32)
    units = len(UNITS)
    last_talls = [tall(UNITS[-1][2])] * 2 + [kv_tall] * 2
    mid_shapes = (
        [pltpu.VMEM((WIN, KV_COLS), BF16)] * 2
        + [bias(2), bias(3), pltpu.VMEM((len(BLOCKS), 8, CW), F32)]
        + [pltpu.VMEM((WIN, LAST_COLS), BF16)] * 2
        + [pltpu.VMEM((CAP, EARLY_COLS), BF16)] * 2
        + [pltpu.VMEM((CAP, EARLY_KV), BF16)] * 2
        + last_talls
    )
    near = [pltpu.VMEM((WIN, count * HEAD_DIM), BF16) for _, _, count in UNITS[:-1] for _ in range(2)]
    talls = [tall(count) for _, _, count in UNITS[:-1] for _ in range(2)]
    dma = pltpu.SemaphoreType.DMA
    mid = pl.pallas_call(
        functools.partial(exchange_kernel, devices),
        out_shape=mid_shapes,
        in_specs=[any_spec] * 4 + [smem] * 3,
        out_specs=[vmem] * len(mid_shapes),
        scratch_shapes=[bias(0), bias(1)]
        + near
        + talls
        + [kv_tall] * (2 * (KV_HEADS - 1))
        + [dma((units, 2, 2)), dma((units, 2, 2)), dma((units, 2)), dma((2, 2)), dma((2, 2)), dma((2,))],
        compiler_params=pltpu.CompilerParams(
            collective_id=0, has_side_effects=True, vmem_limit_bytes=40 << 20
        ),
        name="exchange",
    )(q, g, k, v, lens, owners, table)
    mid = [pltpu.with_memory_space_constraint(x, pltpu.VMEM) for x in mid]
    shapes = [(CAP, w) for w in (HEADS * HEAD_DIM,) * 2 + (KV_COLS,) * 2]
    return tuple(
        pl.pallas_call(
            finish_kernel,
            out_shape=[pltpu.HBM(s, BF16) for s in shapes],
            in_specs=[smem] * 2 + [vmem] * len(mid),
            out_specs=[any_spec] * 4,
            scratch_shapes=[pltpu.VMEM((CAP, LAST_COLS), BF16)] * 2
            + [pltpu.VMEM((CAP, HEAD_DIM), BF16)] * 2
            + last_talls
            + [dma((5, 2)), dma((4,))],
            compiler_params=pltpu.CompilerParams(vmem_limit_bytes=24 << 20),
            name="finish",
        )(lens, owners, *mid)
    )


def solution(mesh):
    rows = P(("dp", "seq"), None)
    return jax.shard_map(
        functools.partial(local, mesh.shape["seq"]),
        mesh=mesh,
        in_specs=(rows, rows, rows, rows, P("dp"), P("dp"), P("dp", None)),
        out_specs=(rows, rows, rows, rows),
        check_vma=False,
    )
```

time: 40.6 us -> 36.7 us (0.904)
  the two profiles are of different devices: /device:TPU:32 before, /device:TPU:174 now
where the time goes in v3:
time: 36.7 us; the launch traced here: 36.5 us
  Pallas kernels  35.7 us (97%)
  between operations  0.8 us (2%)
    pallas_call x1, Pallas kernels, local(): pl.pallas_call(functools.partial(exchange_kernel, devices), out_shape=mid...  32 us
    pallas_call x1, Pallas kernels, local(): pl.pallas_call(finish_kernel, out_shape=[pltpu.HBM(s, BF16) for s in shap...  3.67 us

profile of v3, /device:TPU:174, one launch (start us, length us, event | category | flops | bytes accessed | tf_op | source)
XLA Modules:
  0.0 36.5 jit_solution(11444870446337404457)
XLA Ops:
  0.6 32.0 %exchange.1 = (bf16[192,1024]{1,0:T(8,128)(2,1)S(1)}, bf16[192,1024]{1,0:T(8,128)(2,1)S(1)}, f32[192,256]{1,0:T(8,128)S(1)}, f32[32,256]{1,0:T(8,128)S(1)}, f32[...) custom-call(bf16[128,8192]{1,0:T(8,128)(2,1)} %refs_0_.1, ...), custom_call_target="tpu_custom_call" | custom-call | tf_op jit(solution)/shard_map/exchange/pallas_call | solution.py:401
  32.7 3.7 %finish.1 = (bf16[192,8192]{1,0:T(8,128)(2,1)}, bf16[192,8192]{1,0:T(8,128)(2,1)}, bf16[192,1024]{1,0:T(8,128)(2,1)}, bf16[192,1024]{1,0:T(8,128)(2,1)}) custom-call(s32[32]{0:T(128)} %lens.1, s32[32]{0:T(128)} %owners.1, bf16[192,1024]{1,0:T(8,128)(2,1)S(1)} %get-tuple-element.19.kw, bf16[192,1024]{1,0:T(8,128)(2,1)S(1)} %get-tuple-element.20.vw, ...), custom_call_target="tpu_custom_call" | custom-call | tf_op jit(solution)/shard_map/finish/pallas_call | solution.py:419

commit v4 on v3

v4 whole, which is shorter than its diff:
```python
import functools

import jax
import jax.numpy as jnp
from jax import lax
from jax.experimental import pallas as pl
from jax.experimental.pallas import tpu as pltpu
from jax.sharding import PartitionSpec as P

HEADS = 64
KV_HEADS = 8
HEAD_DIM = 128
BLOCK = 128
CAP = 192
HALO = 32
TOK = 128
WIN = TOK + 2 * HALO
GROUP = HEADS // KV_HEADS
GCOLS = GROUP * HEAD_DIM
QB = 64
CHUNK_HEADS = 4
CW = CHUNK_HEADS * QB
OWN_BLOCKS = ((HALO + QB, QB, 0, HALO + 2 * QB), (HALO, QB, 0, HALO + QB))
AFTER = 2
LENT = 3
BLOCKS = OWN_BLOCKS + ((HALO + TOK, HALO, 0, WIN), (TOK, HALO, TOK, HALO + TOK))
ROW = 4
TALL = CAP + 2 * HALO
INV_ROOT = HEAD_DIM**-0.5
LOG2E = 1.4426950408889634
FAR = -1e30
MESH = pl.DeviceIdType.MESH
BF16 = jnp.bfloat16
F32 = jnp.float32


def dot(a, b, dims):
    return lax.dot_general(a, b, (dims, ((), ())), preferred_element_type=F32)


def clear(tall_refs):
    for ref in tall_refs:
        tail = ref.shape[:-2] + (TALL - WIN, HEAD_DIM)
        ref[..., WIN:TALL, :] = jnp.zeros(tail, F32)


def prepare(me, devices, len_ref, own_ref, table_ref, biases, owned):
    docs = len_ref.shape[0]
    base = me * TOK - HALO
    key_pos = base + lax.broadcasted_iota(jnp.int32, (WIN, 128), 0)
    lane = lax.broadcasted_iota(jnp.int32, (8, CW), 1)
    query_pos = [base + first + lane % count for first, count, _, _ in BLOCKS]

    def one(n, carry):
        start, first, count, lent, key_doc, query_doc = carry
        length = len_ref[n]
        owner = own_ref[n]
        key_doc = key_doc + jnp.where(key_pos >= start, 1, 0)
        query_doc = tuple(
            d + jnp.where(p >= start, 1, 0) for d, p in zip(query_doc, query_pos)
        )
        first = first + jnp.where(owner < me, length, 0)
        count = count + jnp.where(owner == me, length, 0)
        lent = lent + jnp.where(owner == me + 1, length, 0)
        return (start + length, first, count, lent, key_doc, query_doc)

    zero = jnp.int32(0)
    _, first, count, lent, key_doc, query_doc = lax.fori_loop(
        0,
        docs,
        one,
        (
            zero,
            zero,
            zero,
            zero,
            jnp.zeros((WIN, 128), jnp.int32),
            tuple(jnp.zeros((8, CW), jnp.int32) for _ in BLOCKS),
        ),
    )
    before = jnp.maximum(me - 1, 0)
    after = jnp.minimum(me + 1, devices - 1)
    own_before = table_ref[me, before]
    after_own = table_ref[after, me]
    after_before = table_ref[after, before]
    key_pos2 = jnp.concatenate([key_pos] * (CW // 128), axis=1)
    key_doc2 = jnp.concatenate([key_doc] * (CW // 128), axis=1)
    for b, (_, _, low, high) in enumerate(BLOCKS):
        kp, kd = key_pos2[low:high], key_doc2[low:high]
        qp, qd = query_pos[b][:1], query_doc[b][:1]
        key_block = (kp + BLOCK) // BLOCK - me
        query_block = (qp + BLOCK) // BLOCK - me
        linked = jnp.where(
            query_block == 1,
            jnp.where(key_block == 0, own_before, 1),
            jnp.where(
                query_block == 2,
                jnp.where(key_block == 0, after_before, jnp.where(key_block == 1, after_own, 1)),
                1,
            ),
        )
        allowed = (kd == qd) & (kp <= qp) & (linked == 1)
        biases[b][...] = jnp.where(allowed, 0.0, FAR)
        begin, size = (first + count, lent) if b == LENT else (first, count)
        inside = (query_pos[b] >= begin) & (query_pos[b] < begin + size)
        owned[b] = jnp.where(inside, 1.0, 0.0)
    return jnp.clip(first - base, 0, 2 * HALO)


def head_rows(ref, n):
    cols = slice(n * HEAD_DIM, (n + 1) * HEAD_DIM)
    return lambda low, high: ref[low:high, cols]


def scores_of(job, q, g, k, v):
    b, heads = job
    first, count, low, high = BLOCKS[b]
    span = slice(first, first + count)
    qs = jnp.concatenate([q[span, h * HEAD_DIM : (h + 1) * HEAD_DIM] for h in heads], axis=0)
    gs = jnp.concatenate([g[span, h * HEAD_DIM : (h + 1) * HEAD_DIM] for h in heads], axis=0)
    return dot(k(low, high), qs, ((1,), (1,))), dot(v(low, high), gs, ((1,), (1,))), qs, gs


def softmax_of(job, scores, prob_grad, biases, owned):
    b, heads = job
    width = BLOCKS[b][1] * len(heads)
    scores = scores * (INV_ROOT * LOG2E) + biases[b][:, 0:width]
    highest = jnp.max(scores, axis=0, keepdims=True)
    raised = jnp.exp2(scores - highest)
    total = jnp.sum(raised, axis=0, keepdims=True)
    prob = raised * (owned[b, 0:1, 0:width] / total)
    delta = jnp.sum(prob * prob_grad, axis=0, keepdims=True)
    return prob.astype(BF16), (prob * (prob_grad - delta)).astype(BF16)


def query_rows(half, score_grad, first, count, heads, keys, values, out_tall, dq_tall):
    span = slice(first, first + count)
    out = dot(half, values, ((0,), (0,)))
    dq = dot(score_grad, keys, ((0,), (0,))) * INV_ROOT
    for i, h in enumerate(heads):
        out_tall[h, span, :] = out[i * count : (i + 1) * count]
        dq_tall[h, span, :] = dq[i * count : (i + 1) * count]


def key_terms(half, score_grad, qs, gs):
    return dot(score_grad, qs, ((1,), (0,))), dot(half, gs, ((1,), (0,)))


def run_jobs(jobs, fresh_rows, q, g, k, v, biases, owned, out_tall, dq_tall, dk_tall, dv_tall):
    first = [scores_of(job, q, g, k, v) for job in jobs]
    second = [softmax_of(job, f[0], f[1], biases, owned) for job, f in zip(jobs, first)]
    sums = {}
    for (b, heads), (_, _, qs, gs), (half, score_grad) in zip(jobs, first, second):
        start, count, low, high = BLOCKS[b]
        query_rows(half, score_grad, start, count, heads, k(low, high), v(low, high), out_tall, dq_tall)
        dk, dv = key_terms(half, score_grad, qs, gs)
        old = sums.get(b)
        sums[b] = (dk, dv) if old is None else (old[0] + dk, old[1] + dv)
    for b, (dk, dv) in sums.items():
        rows = BLOCKS[b][3]
        old = min(rows, fresh_rows)
        if old:
            dk_tall[0:old, :] += dk[0:old]
            dv_tall[0:old, :] += dv[0:old]
        if old < rows:
            dk_tall[old:rows, :] = dk[old:rows]
            dv_tall[old:rows, :] = dv[old:rows]
        fresh_rows = max(fresh_rows, rows)


def own_pass(fresh, q, *rest):
    count = q.shape[1] // HEAD_DIM
    jobs = [
        (b, range(c, c + CHUNK_HEADS))
        for b in range(len(OWN_BLOCKS))
        for c in range(0, count, CHUNK_HEADS)
    ]
    run_jobs(jobs, 0 if fresh else WIN, q, *rest)


def lend_pass(q, g, k, v, biases, owned, parcel):
    job = (LENT, range(q.shape[1] // HEAD_DIM))
    scores, prob_grad, qs, gs = scores_of(job, q, g, k, v)
    half, score_grad = softmax_of(job, scores, prob_grad, biases, owned)
    width = half.shape[1]
    parcel[:, 0:width] = half
    parcel[:, width : 2 * width] = score_grad
    dk, dv = key_terms(half, score_grad, qs, gs)
    parcel[:, 2 * width : 2 * width + HEAD_DIM] = dk.astype(BF16)
    parcel[:, 2 * width + HEAD_DIM : 2 * width + 2 * HEAD_DIM] = dv.astype(BF16)


def halo_pass(fresh, q, g, k, v, biases, owned, out_tall, dq_tall, dk_tall, dv_tall, parcel):
    heads = range(q.shape[1] // HEAD_DIM)
    width = HALO * len(heads)
    query_rows(
        parcel[:, 0:width], parcel[:, width : 2 * width], 0, HALO, heads, k(0, HALO), v(0, HALO), out_tall, dq_tall
    )
    run_jobs(
        [(AFTER, heads)], HALO + TOK if fresh else WIN, q, g, k, v, biases, owned, out_tall, dq_tall, dk_tall, dv_tall
    )
    dk_tall[0:HALO, :] += parcel[:, 2 * width : 2 * width + HEAD_DIM].astype(F32)
    dv_tall[0:HALO, :] += parcel[:, 2 * width + HEAD_DIM : 2 * width + 2 * HEAD_DIM].astype(F32)


def shift_queries(shift, out_tall, dq_tall, out, dq):
    rows = pl.ds(shift, CAP)
    for h in range(out.shape[1] // HEAD_DIM):
        cols = slice(h * HEAD_DIM, (h + 1) * HEAD_DIM)
        out[:, cols] = out_tall[h, rows, :].astype(BF16)
        dq[:, cols] = dq_tall[h, rows, :].astype(BF16)


def shift_keys(shift, dk_tall, dv_tall, dk, dv):
    rows = pl.ds(shift, CAP)
    dk[...] = (dk_tall[rows, :] * INV_ROOT).astype(BF16)
    dv[...] = dv_tall[rows, :].astype(BF16)


AHEAD = 7
LEND_CUTS = (4, 6)
RELAY_AT = (3, 6)
RELAYED = 6
UNITS = [(n, 0, GROUP) for n in range(KV_HEADS - 1)] + [
    (KV_HEADS - 1, 0, GROUP // 2),
    (KV_HEADS - 1, GROUP // 2, GROUP // 2),
]
LAST_COLS = UNITS[-1][2] * HEAD_DIM
EARLY_COLS = HEADS * HEAD_DIM - LAST_COLS
KV_COLS = KV_HEADS * HEAD_DIM
EARLY_KV = KV_COLS - HEAD_DIM


def unit_cols(u):
    n, first, count = UNITS[u]
    return pl.ds(n * GCOLS + first * HEAD_DIM, count * HEAD_DIM)


def kv_cols(n):
    return pl.ds(n * HEAD_DIM, HEAD_DIM)


def exchange_kernel(devices, *refs):
    refs = list(refs)

    def take(count):
        taken = refs[:count]
        del refs[:count]
        return taken

    def pairs(count):
        return [take(2) for _ in range(count)]

    units = len(UNITS)
    early = units - 1
    q, g, k, v, lens, owners, table = take(7)
    kw, vw, bias_after, owned, last_q, last_g, done_o, done_q, done_k, done_v = take(10)
    last_talls, last_kv_talls = pairs(2)
    last_lent = take(1)
    biases = take(2) + [bias_after] + take(1)
    near = pairs(early) + [(last_q, last_g)]
    talls = pairs(early) + [last_talls]
    kv_talls = pairs(KV_HEADS - 1) + [last_kv_talls]
    lent = take(early) + last_lent
    lend = take(units)
    relay = pairs(2)
    send, recv, load, kv_send, kv_recv, kv_load, lend_send, lend_recv, relay_send, relay_recv = take(10)
    dp = lax.axis_index("dp")
    me = lax.axis_index("seq")
    x = lax.rem(me, ROW)
    has = (me < devices - 1, me > 0)
    peer = (jnp.minimum(me + 1, devices - 1), jnp.maximum(me - 1, 0))
    near_row = me - x + lax.rem(x + 1, ROW)
    above = (x == 0) | ((x == 1) & (me < devices - ROW))
    below = (x == ROW - 1) | ((x == 0) & (me > 0))
    relay_to = jnp.maximum(jnp.where(x == 0, me - 3, near_row), 0)
    relayed = (me != 0, me != devices - 3, me != devices - 2, me != devices - 1)

    def remote(src, dst, target, send_sem, recv_sem):
        return pltpu.make_async_remote_copy(
            src_ref=src, dst_ref=dst, send_sem=send_sem, recv_sem=recv_sem, device_id=(dp, target), device_id_type=MESH
        )

    def hop(src, cols, dst, side, sems):
        rows = pl.ds(TOK - HALO, HALO) if side == 0 else pl.ds(0, HALO)
        there = pl.ds(0, HALO) if side == 0 else pl.ds(HALO + TOK, HALO)
        return remote(src.at[rows, cols], dst.at[there, :], peer[side], *sems)

    def own(src, cols, dst, sem):
        return pltpu.make_async_copy(src.at[:, cols], dst.at[pl.ds(HALO, TOK), :], sem)

    every = pl.ds(0, KV_COLS)
    kv = ((k, kw), (v, vw))
    kv_hops = [
        [hop(src, every, dst, side, (kv_send.at[a, side], kv_recv.at[a, side])) for a, (src, dst) in enumerate(kv)]
        for side in range(2)
    ]
    kv_own = [own(src, every, dst, kv_load.at[a]) for a, (src, dst) in enumerate(kv)]
    hops = [
        [
            hop(src, unit_cols(u), near[u][a], 1, (send.at[u, a], recv.at[u, a]))
            for a, src in enumerate((q, g))
            if u != RELAYED
        ]
        for u in range(units)
    ]
    lends = [
        [remote(lend[u], lent[u], peer[0], lend_send.at[u], lend_recv.at[u])] for u in range(units)
    ]
    after = pl.ds(HALO + TOK, HALO)
    relays = [
        [
            remote(src.at[pl.ds(0, HALO), unit_cols(RELAYED)], relay[0][a], relay_to, relay_send.at[0, a], relay_recv.at[0, a])
            for a, src in enumerate((q, g))
        ],
        [remote(relay[0][a], relay[1][a], near_row, relay_send.at[1, a], relay_recv.at[1, a]) for a in range(2)],
        [
            remote(relay[1][a], near[RELAYED][a].at[after, :], near_row, relay_send.at[2, a], relay_recv.at[2, a])
            for a in range(2)
        ],
    ]
    owns = [
        [own(src, unit_cols(u), near[u][a], load.at[u, a]) for a, src in enumerate((q, g))]
        for u in range(units)
    ]

    barrier = pltpu.get_barrier_semaphore()
    greet = ((has[0], peer[0]), (has[1], peer[1]), (above, jnp.minimum(me + 3, devices - 1)), (below, jnp.maximum(me - 3, 0)))
    peers = jnp.int32(0)
    for meets, other in greet:
        peers = peers + jnp.where(meets, 1, 0)

        @pl.when(meets)
        def _():
            pl.semaphore_signal(barrier, inc=1, device_id=(dp, other), device_id_type=MESH)

    pl.semaphore_wait(barrier, peers)

    def start(copies):
        for copy in copies:
            copy.start()

    def arrive(copies, sends, receives):
        @pl.when(sends)
        def _():
            for copy in copies:
                copy.wait_send()

        @pl.when(receives)
        def _():
            for copy in copies:
                copy.wait_recv()

    for side in (0, 1):

        @pl.when(has[side])
        def _():
            start(kv_hops[side])

    @pl.when(relayed[0])
    def _():
        start(relays[0])

    for u in range(units):
        if u != RELAYED:

            @pl.when(has[1])
            def _():
                start(hops[u])

    start(kv_own)
    for copies in owns:
        start(copies)

    def fill(ref, rows):
        ref[rows, :] = jnp.zeros((HALO, ref.shape[1]), ref.dtype)

    @pl.when(me == 0)
    def _():
        for ref in lent + [kw, vw]:
            fill(ref, pl.ds(0, HALO))

    @pl.when(me == devices - 1)
    def _():
        for ref in [r for pair in near for r in pair] + [kw, vw]:
            fill(ref, after)

    shift = prepare(me, devices, lens, owners, table, biases, owned)
    for pair in talls + kv_talls:
        clear(pair)

    def columns(u):
        return head_rows(kw, UNITS[u][0]), head_rows(vw, UNITS[u][0])

    def operands(u):
        n, first, _ = UNITS[u]
        return (first == 0, *near[u], *columns(u), biases, owned, *talls[u], *kv_talls[n])

    def lend_rows(u):
        for copy in owns[u]:
            copy.wait()
        lend_pass(*near[u], *columns(u), biases, owned, lend[u])

    def lend_out(first, last):
        @pl.when(has[0])
        def _():
            for copies in lends[first:last]:
                start(copies)

    for copy in kv_own:
        copy.wait()
    for u in range(units):
        lend_rows(u)
    lend_out(0, LEND_CUTS[0])
    arrive(kv_hops[0], has[0], has[1])
    for u in range(RELAY_AT[0]):
        own_pass(*operands(u))
    arrive(relays[0], relayed[0], relayed[1])

    @pl.when(relayed[1])
    def _():
        start(relays[1])

    lend_out(*LEND_CUTS[0:2])
    for u in range(*RELAY_AT):
        own_pass(*operands(u))
    arrive(relays[1], relayed[1], relayed[2])

    @pl.when(relayed[2])
    def _():
        start(relays[2])

    lend_out(LEND_CUTS[1], units)
    for u in range(RELAY_AT[1], AHEAD):
        own_pass(*operands(u))
    arrive(kv_hops[1], has[1], has[0])
    for u, (n, first, count) in enumerate(UNITS):
        if u + AHEAD < units:
            own_pass(*operands(u + AHEAD))
        if u == RELAYED:
            arrive(relays[2], relayed[2], relayed[3])
        else:
            arrive(hops[u], has[1], has[0])
        arrive(lends[u], has[0], has[1])
        if u == early:
            break
        halo_pass(*operands(u), lent[u])
        shift_queries(shift, *talls[u], done_o.at[:, unit_cols(u)], done_q.at[:, unit_cols(u)])
        if first + count == GROUP:
            shift_keys(shift, *kv_talls[n], done_k.at[:, kv_cols(n)], done_v.at[:, kv_cols(n)])


def finish_kernel(lens, owners, kw, vw, bias_after, owned, last_q, last_g, done_o, done_q, done_k, done_v,
                  out_part, dq_part, dk_part, dv_part, parcel, out, dq, dk, dv, stage_o, stage_q, stage_k, stage_v,
                  out_tall, dq_tall, dk_tall, dv_tall, flush, store):
    me = lax.axis_index("seq")
    pieces = 4
    width = EARLY_COLS // pieces
    moves = []
    for p in range(pieces):
        cols = pl.ds(p * width, width)
        moves.append(pltpu.make_async_copy(done_o.at[:, cols], out.at[:, cols], flush.at[p, 0]))
        moves.append(pltpu.make_async_copy(done_q.at[:, cols], dq.at[:, cols], flush.at[p, 1]))
    cols = pl.ds(0, EARLY_KV)
    moves.append(pltpu.make_async_copy(done_k, dk.at[:, cols], flush.at[pieces, 0]))
    moves.append(pltpu.make_async_copy(done_v, dv.at[:, cols], flush.at[pieces, 1]))
    for move in moves:
        move.start()

    def one(n, first):
        return first + jnp.where(owners[n] < me, lens[n], 0)

    shift = lax.fori_loop(0, lens.shape[0], one, jnp.int32(0)) - (me * TOK - HALO)
    shift = jnp.clip(shift, 0, 2 * HALO)
    middle = slice(HALO, HALO + TOK)
    for ref, part in ((out_tall, out_part), (dq_tall, dq_part)):
        ref[:, middle, :] = part[:, middle, :]
    clear((out_tall, dq_tall))
    dk_tall[...] = dk_part[...]
    dv_tall[...] = dv_part[...]
    n = KV_HEADS - 1
    halo_pass(
        False, last_q, last_g, head_rows(kw, n), head_rows(vw, n), (None, None, bias_after), owned,
        out_tall, dq_tall, dk_tall, dv_tall, parcel,
    )
    shift_queries(shift, out_tall, dq_tall, stage_o, stage_q)
    shift_keys(shift, dk_tall, dv_tall, stage_k, stage_v)
    cols = pl.ds(EARLY_COLS, LAST_COLS)
    rest = [
        pltpu.make_async_copy(stage_o, out.at[:, cols], store.at[0]),
        pltpu.make_async_copy(stage_q, dq.at[:, cols], store.at[1]),
        pltpu.make_async_copy(stage_k, dk.at[:, kv_cols(n)], store.at[2]),
        pltpu.make_async_copy(stage_v, dv.at[:, kv_cols(n)], store.at[3]),
    ]
    for move in rest:
        move.start()
    for move in moves + rest:
        move.wait()


def local(devices, q, k, v, g, lens, owners, table):
    any_spec = pl.BlockSpec(memory_space=pl.ANY)
    vmem = pl.BlockSpec(memory_space=pltpu.VMEM)
    smem = pl.BlockSpec(memory_space=pltpu.SMEM)
    q, k, v, g, lens, owners, table = [
        pltpu.with_memory_space_constraint(x, pltpu.HBM) for x in (q, k, v, g, lens, owners, table)
    ]
    def tall(count):
        return pltpu.VMEM((count, TALL, HEAD_DIM), F32)

    def bias(b):
        return pltpu.VMEM((BLOCKS[b][3] - BLOCKS[b][2], CW), F32)

    def lent(u):
        return pltpu.VMEM((HALO, 2 * HALO * UNITS[u][2] + 2 * HEAD_DIM), BF16)

    kv_tall = pltpu.VMEM((TALL, HEAD_DIM), F32)
    units = len(UNITS)
    last_talls = [tall(UNITS[-1][2])] * 2 + [kv_tall] * 2
    mid_shapes = (
        [pltpu.VMEM((WIN, KV_COLS), BF16)] * 2
        + [bias(AFTER), pltpu.VMEM((len(BLOCKS), 8, CW), F32)]
        + [pltpu.VMEM((WIN, LAST_COLS), BF16)] * 2
        + [pltpu.VMEM((CAP, EARLY_COLS), BF16)] * 2
        + [pltpu.VMEM((CAP, EARLY_KV), BF16)] * 2
        + last_talls
        + [lent(units - 1)]
    )
    near = [pltpu.VMEM((WIN, count * HEAD_DIM), BF16) for _, _, count in UNITS[:-1] for _ in range(2)]
    talls = [tall(count) for _, _, count in UNITS[:-1] for _ in range(2)]
    dma = pltpu.SemaphoreType.DMA
    mid = pl.pallas_call(
        functools.partial(exchange_kernel, devices),
        out_shape=mid_shapes,
        in_specs=[any_spec] * 4 + [smem] * 3,
        out_specs=[vmem] * len(mid_shapes),
        scratch_shapes=[bias(0), bias(1), bias(LENT)]
        + near
        + talls
        + [kv_tall] * (2 * (KV_HEADS - 1))
        + [lent(u) for u in range(units - 1)]
        + [lent(u) for u in range(units)]
        + [pltpu.VMEM((HALO, GCOLS), BF16)] * 4
        + [dma((units, 2))] * 3
        + [dma((2, 2))] * 2
        + [dma((2,))]
        + [dma((units,))] * 2
        + [dma((3, 2))] * 2,
        compiler_params=pltpu.CompilerParams(
            collective_id=0, has_side_effects=True, vmem_limit_bytes=40 << 20
        ),
        name="exchange",
    )(q, g, k, v, lens, owners, table)
    mid = [pltpu.with_memory_space_constraint(x, pltpu.VMEM) for x in mid]
    shapes = [(CAP, w) for w in (HEADS * HEAD_DIM,) * 2 + (KV_COLS,) * 2]
    return tuple(
        pl.pallas_call(
            finish_kernel,
            out_shape=[pltpu.HBM(s, BF16) for s in shapes],
            in_specs=[smem] * 2 + [vmem] * len(mid),
            out_specs=[any_spec] * 4,
            scratch_shapes=[pltpu.VMEM((CAP, LAST_COLS), BF16)] * 2
            + [pltpu.VMEM((CAP, HEAD_DIM), BF16)] * 2
            + last_talls
            + [dma((5, 2)), dma((4,))],
            compiler_params=pltpu.CompilerParams(vmem_limit_bytes=24 << 20),
            name="finish",
        )(lens, owners, *mid)
    )


def solution(mesh):
    rows = P(("dp", "seq"), None)
    return jax.shard_map(
        functools.partial(local, mesh.shape["seq"]),
        mesh=mesh,
        in_specs=(rows, rows, rows, rows, P("dp"), P("dp"), P("dp", None)),
        out_specs=(rows, rows, rows, rows),
        check_vma=False,
    )
```

time: 36.7 us -> 34.1 us (0.929)
  Pallas kernels: 35.7 us -> 33.4 us
    pallas_call x1, Pallas kernels: 32 us -> 29.7 us  [local(): pl.pallas_call(functools.partial(exchange_kernel, devices), out_shape=mid...]
where the time goes in v4:
time: 34.1 us; the launch traced here: 34 us
  Pallas kernels  33.4 us (98%)
  between operations  0.64 us (2%)
    pallas_call x1, Pallas kernels, local(): pl.pallas_call(functools.partial(exchange_kernel, devices), out_shape=mid...  29.7 us
    pallas_call x1, Pallas kernels, local(): pl.pallas_call(finish_kernel, out_shape=[pltpu.HBM(s, BF16) for s in shap...  3.67 us

profile of v4, /device:TPU:174, one launch (start us, length us, event | category | flops | bytes accessed | tf_op | source)
XLA Modules:
  0.0 34.0 jit_solution(14024769799373882393)
XLA Ops:
  0.6 29.7 %exchange.1 = (bf16[192,1024]{1,0:T(8,128)(2,1)S(1)}, bf16[192,1024]{1,0:T(8,128)(2,1)S(1)}, f32[192,256]{1,0:T(8,128)S(1)}, f32[4,8,256]{2,1,0:T(8,128)S(1)}, b...) custom-call(bf16[128,8192]{1,0:T(8,128)(2,1)} %refs_0_.1, ...), custom_call_target="tpu_custom_call" | custom-call | tf_op jit(solution)/shard_map/exchange/pallas_call | solution.py:532
  30.3 3.7 %finish.1 = (bf16[192,8192]{1,0:T(8,128)(2,1)}, bf16[192,8192]{1,0:T(8,128)(2,1)}, bf16[192,1024]{1,0:T(8,128)(2,1)}, bf16[192,1024]{1,0:T(8,128)(2,1)}) custom-call(s32[32]{0:T(128)} %lens.1, s32[32]{0:T(128)} %owners.1, bf16[192,1024]{1,0:T(8,128)(2,1)S(1)} %get-tuple-element.19.kw, bf16[192,1024]{1,0:T(8,128)(2,1)S(1)} %get-tuple-element.20.vw, ...), custom_call_target="tpu_custom_call" | custom-call | tf_op jit(solution)/shard_map/finish/pallas_call | solution.py:557

commit v5 on v4

--- a/solution.py
+++ b/solution.py
@@ -171,7 +171,7 @@
 def own_pass(fresh, q, *rest):
     count = q.shape[1] // HEAD_DIM
     jobs = [
-        (b, range(c, c + CHUNK_HEADS))
+        (b, range(c, min(c + CHUNK_HEADS, count)))
         for b in range(len(OWN_BLOCKS))
         for c in range(0, count, CHUNK_HEADS)
     ]
@@ -220,10 +220,11 @@
 AHEAD = 7
 LEND_CUTS = (4, 6)
 RELAY_AT = (3, 6)
-RELAYED = 6
+RELAYED = (6, 7)
+LAST_HEADS = 4
 UNITS = [(n, 0, GROUP) for n in range(KV_HEADS - 1)] + [
-    (KV_HEADS - 1, 0, GROUP // 2),
-    (KV_HEADS - 1, GROUP // 2, GROUP // 2),
+    (KV_HEADS - 1, 0, GROUP - LAST_HEADS),
+    (KV_HEADS - 1, GROUP - LAST_HEADS, LAST_HEADS),
 ]
 LAST_COLS = UNITS[-1][2] * HEAD_DIM
 EARLY_COLS = HEADS * HEAD_DIM - LAST_COLS
@@ -263,7 +264,7 @@
     kv_talls = pairs(KV_HEADS - 1) + [last_kv_talls]
     lent = take(early) + last_lent
     lend = take(units)
-    relay = pairs(2)
+    relay = [pairs(len(RELAYED)) for _ in range(2)]
     send, recv, load, kv_send, kv_recv, kv_load, lend_send, lend_recv, relay_send, relay_recv = take(10)
     dp = lax.axis_index("dp")
     me = lax.axis_index("seq")
@@ -275,6 +276,7 @@
     below = (x == ROW - 1) | ((x == 0) & (me > 0))
     relay_to = jnp.maximum(jnp.where(x == 0, me - 3, near_row), 0)
     relayed = (me != 0, me != devices - 3, me != devices - 2, me != devices - 1)
+    relay_when = (relayed, tuple(ok & (x == step) for step, ok in enumerate(relayed)))
 
     def remote(src, dst, target, send_sem, recv_sem):
         return pltpu.make_async_remote_copy(
@@ -300,7 +302,7 @@
         [
             hop(src, unit_cols(u), near[u][a], 1, (send.at[u, a], recv.at[u, a]))
             for a, src in enumerate((q, g))
-            if u != RELAYED
+            if u != RELAYED[0]
         ]
         for u in range(units)
     ]
@@ -308,17 +310,19 @@
         [remote(lend[u], lent[u], peer[0], lend_send.at[u], lend_recv.at[u])] for u in range(units)
     ]
     after = pl.ds(HALO + TOK, HALO)
-    relays = [
-        [
-            remote(src.at[pl.ds(0, HALO), unit_cols(RELAYED)], relay[0][a], relay_to, relay_send.at[0, a], relay_recv.at[0, a])
-            for a, src in enumerate((q, g))
-        ],
-        [remote(relay[0][a], relay[1][a], near_row, relay_send.at[1, a], relay_recv.at[1, a]) for a in range(2)],
-        [
-            remote(relay[1][a], near[RELAYED][a].at[after, :], near_row, relay_send.at[2, a], relay_recv.at[2, a])
-            for a in range(2)
-        ],
-    ]
+    relays = [[[] for _ in RELAYED] for _ in range(3)]
+    for i, u in enumerate(RELAYED):
+        for a, src in enumerate((q, g)):
+            first, second = relay[0][i][a], relay[1][i][a]
+            path = (
+                (src.at[pl.ds(0, HALO), unit_cols(u)], first, relay_to),
+                (first, second, near_row),
+                (second, near[u][a].at[after, :], near_row),
+            )
+            for step, (here, there, target) in enumerate(path):
+                relays[step][i].append(
+                    remote(here, there, target, relay_send.at[step, i, a], relay_recv.at[step, i, a])
+                )
     owns = [
         [own(src, unit_cols(u), near[u][a], load.at[u, a]) for a, src in enumerate((q, g))]
         for u in range(units)
@@ -334,11 +338,11 @@
         def _():
             pl.semaphore_signal(barrier, inc=1, device_id=(dp, other), device_id_type=MESH)
 
-    pl.semaphore_wait(barrier, peers)
-
     def start(copies):
         for copy in copies:
             copy.start()
+
+    pl.semaphore_wait(barrier, peers)
 
     def arrive(copies, sends, receives):
         @pl.when(sends)
@@ -357,14 +361,23 @@
         def _():
             start(kv_hops[side])
 
-    @pl.when(relayed[0])
-    def _():
-        start(relays[0])
-
+    def relay_start(step):
+        for copies, ok in zip(relays[step], relay_when):
+
+            @pl.when(ok[step])
+            def _():
+                start(copies)
+
+    def relay_arrive(step, i):
+        arrive(relays[step][i], relay_when[i][step], relay_when[i][step + 1])
+
+    direct = [has for _ in range(units)]
+    direct[RELAYED[1]] = (has[0] & (x != ROW - 1), has[1] & (x != 0))
+    relay_start(0)
     for u in range(units):
-        if u != RELAYED:
-
-            @pl.when(has[1])
+        if u != RELAYED[0]:
+
+            @pl.when(direct[u][1])
             def _():
                 start(hops[u])
 
@@ -415,21 +428,15 @@
     arrive(kv_hops[0], has[0], has[1])
     for u in range(RELAY_AT[0]):
         own_pass(*operands(u))
-    arrive(relays[0], relayed[0], relayed[1])
-
-    @pl.when(relayed[1])
-    def _():
-        start(relays[1])
-
+    for i in range(len(RELAYED)):
+        relay_arrive(0, i)
+    relay_start(1)
     lend_out(*LEND_CUTS[0:2])
     for u in range(*RELAY_AT):
         own_pass(*operands(u))
-    arrive(relays[1], relayed[1], relayed[2])
-
-    @pl.when(relayed[2])
-    def _():
-        start(relays[2])
-
+    for i in range(len(RELAYED)):
+        relay_arrive(1, i)
+    relay_start(2)
     lend_out(LEND_CUTS[1], units)
     for u in range(RELAY_AT[1], AHEAD):
         own_pass(*operands(u))
@@ -437,10 +444,10 @@
     for u, (n, first, count) in enumerate(UNITS):
         if u + AHEAD < units:
             own_pass(*operands(u + AHEAD))
-        if u == RELAYED:
-            arrive(relays[2], relayed[2], relayed[3])
-        else:
-            arrive(hops[u], has[1], has[0])
+        if u in RELAYED:
+            relay_arrive(2, RELAYED.index(u))
+        if u != RELAYED[0]:
+            arrive(hops[u], direct[u][1], direct[u][0])
         arrive(lends[u], has[0], has[1])
         if u == early:
             break
@@ -454,7 +461,7 @@
                   out_part, dq_part, dk_part, dv_part, parcel, out, dq, dk, dv, stage_o, stage_q, stage_k, stage_v,
                   out_tall, dq_tall, dk_tall, dv_tall, flush, store):
     me = lax.axis_index("seq")
-    pieces = 4
+    pieces = 2
     width = EARLY_COLS // pieces
     moves = []
     for p in range(pieces):
@@ -540,12 +547,12 @@
         + [kv_tall] * (2 * (KV_HEADS - 1))
         + [lent(u) for u in range(units - 1)]
         + [lent(u) for u in range(units)]
-        + [pltpu.VMEM((HALO, GCOLS), BF16)] * 4
+        + [pltpu.VMEM((HALO, UNITS[u][2] * HEAD_DIM), BF16) for _ in range(2) for u in RELAYED for _ in range(2)]
         + [dma((units, 2))] * 3
         + [dma((2, 2))] * 2
         + [dma((2,))]
         + [dma((units,))] * 2
-        + [dma((3, 2))] * 2,
+        + [dma((3, len(RELAYED), 2))] * 2,
         compiler_params=pltpu.CompilerParams(
             collective_id=0, has_side_effects=True, vmem_limit_bytes=40 << 20
         ),
@@ -562,7 +569,7 @@
             scratch_shapes=[pltpu.VMEM((CAP, LAST_COLS), BF16)] * 2
             + [pltpu.VMEM((CAP, HEAD_DIM), BF16)] * 2
             + last_talls
-            + [dma((5, 2)), dma((4,))],
+            + [dma((3, 2)), dma((4,))],
             compiler_params=pltpu.CompilerParams(vmem_limit_bytes=24 << 20),
             name="finish",
         )(lens, owners, *mid)

time: 34.1 us -> 33.8 us (level)
  Pallas kernels: 33.4 us -> 33 us
where the time goes in v5:
time: 33.8 us; the launch traced here: 33.6 us
  Pallas kernels  33 us (98%)
  between operations  0.64 us (2%)
    pallas_call x1, Pallas kernels, local(): pl.pallas_call(functools.partial(exchange_kernel, devices), out_shape=mid...  29.3 us
    pallas_call x1, Pallas kernels, local(): pl.pallas_call(finish_kernel, out_shape=[pltpu.HBM(s, BF16) for s in shap...  3.64 us

profile of v5, /device:TPU:174, one launch (start us, length us, event | category | flops | bytes accessed | tf_op | source)
XLA Modules:
  0.0 33.6 jit_solution(12272416045713869505)
XLA Ops:
  0.6 29.3 %exchange.1 = (bf16[192,1024]{1,0:T(8,128)(2,1)S(1)}, bf16[192,1024]{1,0:T(8,128)(2,1)S(1)}, f32[192,256]{1,0:T(8,128)S(1)}, f32[4,8,256]{2,1,0:T(8,128)S(1)}, b...) custom-call(bf16[128,8192]{1,0:T(8,128)(2,1)} %refs_0_.1, ...), custom_call_target="tpu_custom_call" | custom-call | tf_op jit(solution)/shard_map/exchange/pallas_call | solution.py:539
  30.0 3.6 %finish.1 = (bf16[192,8192]{1,0:T(8,128)(2,1)}, bf16[192,8192]{1,0:T(8,128)(2,1)}, bf16[192,1024]{1,0:T(8,128)(2,1)}, bf16[192,1024]{1,0:T(8,128)(2,1)}) custom-call(s32[32]{0:T(128)} %lens.1, s32[32]{0:T(128)} %owners.1, bf16[192,1024]{1,0:T(8,128)(2,1)S(1)} %get-tuple-element.19.kw, bf16[192,1024]{1,0:T(8,128)(2,1)S(1)} %get-tuple-element.20.vw, ...), custom_call_target="tpu_custom_call" | custom-call | tf_op jit(solution)/shard_map/finish/pallas_call | solution.py:564

commit v6 on v5

--- a/solution.py
+++ b/solution.py
@@ -221,7 +221,7 @@
 LEND_CUTS = (4, 6)
 RELAY_AT = (3, 6)
 RELAYED = (6, 7)
-LAST_HEADS = 4
+LAST_HEADS = 2
 UNITS = [(n, 0, GROUP) for n in range(KV_HEADS - 1)] + [
     (KV_HEADS - 1, 0, GROUP - LAST_HEADS),
     (KV_HEADS - 1, GROUP - LAST_HEADS, LAST_HEADS),

time: 33.8 us -> 35.3 us (1.044)
  the two profiles are of different devices: /device:TPU:174 before, /device:TPU:132 now
where the time goes in v6:
time: 35.3 us; the launch traced here: 35.2 us
  Pallas kernels  34.6 us (98%)
  between operations  0.64 us (2%)
    pallas_call x1, Pallas kernels, local(): pl.pallas_call(functools.partial(exchange_kernel, devices), out_shape=mid...  30.9 us
    pallas_call x1, Pallas kernels, local(): pl.pallas_call(finish_kernel, out_shape=[pltpu.HBM(s, BF16) for s in shap...  3.64 us

profile of v6, /device:TPU:132, one launch (start us, length us, event | category | flops | bytes accessed | tf_op | source)
XLA Modules:
  0.0 35.2 jit_solution(2518976907039502419)
XLA Ops:
  0.6 30.9 %exchange.1 = (bf16[192,1024]{1,0:T(8,128)(2,1)S(1)}, bf16[192,1024]{1,0:T(8,128)(2,1)S(1)}, f32[192,256]{1,0:T(8,128)S(1)}, f32[4,8,256]{2,1,0:T(8,128)S(1)}, b...) custom-call(bf16[128,8192]{1,0:T(8,128)(2,1)} %refs_0_.1, ...), custom_call_target="tpu_custom_call" | custom-call | tf_op jit(solution)/shard_map/exchange/pallas_call | solution.py:539
  31.6 3.6 %finish.1 = (bf16[192,8192]{1,0:T(8,128)(2,1)}, bf16[192,8192]{1,0:T(8,128)(2,1)}, bf16[192,1024]{1,0:T(8,128)(2,1)}, bf16[192,1024]{1,0:T(8,128)(2,1)}) custom-call(s32[32]{0:T(128)} %lens.1, s32[32]{0:T(128)} %owners.1, bf16[192,1024]{1,0:T(8,128)(2,1)S(1)} %get-tuple-element.19.kw, bf16[192,1024]{1,0:T(8,128)(2,1)S(1)} %get-tuple-element.20.vw, ...), custom_call_target="tpu_custom_call" | custom-call | tf_op jit(solution)/shard_map/finish/pallas_call | solution.py:564
